TPU v7x, 32 devices: a whole 2x2x4 slice. The times are simulated.
32 devices in a mesh: dp: 4 (over x, core), fsdp: 8 (over z, y).
Axes of the slice: x: 2, y: 2, z: 4, core: 2. Of those that a mesh axis runs over, the one named last changes fastest.
Arguments:
- attention_output_rows: bfloat16 [8192, 1536], P(('dp', 'fsdp')), may hold values from -6 to 6
- cotangent: bfloat16 [8192, 3072], P(('dp', 'fsdp')), may hold values from -6 to 6
- quantized_weight_codes: bfloat16 [1536, 3072], P('fsdp'), may hold values from -1 to 1
- shard_absolute_maximum: bfloat16 [8], P('fsdp'), may hold values from 0.019897461 to 0.079589844
- adapter_down_weight: bfloat16 [1536, 128], P('fsdp'), may hold values from -0.15625 to 0.15625
- adapter_up_weight: bfloat16 [128, 3072], P(None, 'fsdp'), may hold values from -0.5 to 0.5
- timestep_gate_weight: bfloat16 [256, 3072], P('fsdp'), may hold values from -0.375 to 0.375
- timesteps: int32 [2], replicated, may hold values from 0 to 999
Outputs:
- mixed_update: bfloat16 [8192, 3072], P(('dp', 'fsdp'))
- attention_output_gradient: bfloat16 [8192, 1536], P(('dp', 'fsdp'))
- down_grad: float32 [1536, 128], P('fsdp')
- scaled_up_gradient: float32 [128, 3072], P(None, 'fsdp')
All inputs are finite; a program needn't handle non-finite values.
Results may differ from a plain program's by a relative error of at most 0.0075.
Values may be sent and summed in bfloat16 or wider, within the bound.
A program may use at most 64 MiB of HBM per device.

v0:
```python
import math

import jax
import jax.numpy as jnp
from jax import lax
from jax.sharding import PartitionSpec as P

FREQ = 256
PATCHES = 4096


adapter_scale_factor = 0.5


def per_device(
    attention_output_rows,
    cotangent,
    quantized_weight_codes,
    shard_absolute_maximum,
    adapter_down_weight,
    adapter_up_weight,
    timestep_gate_weight,
    timesteps,
):
    row_count = attention_output_rows.shape[0]
    dp_count = lax.axis_size("dp")
    fsdp_count = lax.axis_size("fsdp")
    amax_rows = jnp.broadcast_to(shard_absolute_maximum, (quantized_weight_codes.shape[0],))
    all_codes, scales = (
        lax.all_gather(quantized_weight_codes, "fsdp", axis=0, tiled=True),
        lax.all_gather(amax_rows, "fsdp", axis=0, tiled=True),
    )
    weight = (all_codes.astype(jnp.float32) * scales.astype(jnp.float32)[:, None]).astype(
        jnp.bfloat16
    )
    down_all, gathered_up_weight, gate_all = (
        lax.all_gather(adapter_down_weight, "fsdp", axis=0, tiled=True),
        lax.all_gather(adapter_up_weight, "fsdp", axis=1, tiled=True),
        lax.all_gather(timestep_gate_weight, "fsdp", axis=0, tiled=True),
    )
    sample_index = (
        (lax.axis_index("dp") * fsdp_count + lax.axis_index("fsdp")) * row_count // PATCHES
    )
    step_value = lax.dynamic_slice_in_dim(timesteps, sample_index, 1)
    half_freq = FREQ // 2
    frequency = jnp.exp(-math.log(10000.0) * jnp.arange(half_freq, dtype=jnp.float32) / half_freq)
    phase_angle = step_value.astype(jnp.float32)[:, None] * frequency[None, :]
    features = jnp.concatenate([jnp.cos(phase_angle), jnp.sin(phase_angle)], axis=1).astype(
        jnp.bfloat16
    )
    gate_row = jnp.dot(features, gate_all, preferred_element_type=jnp.float32)
    bottleneck_activation = jnp.dot(
        attention_output_rows, down_all, preferred_element_type=jnp.float32
    ).astype(jnp.bfloat16)
    projection_output = jnp.dot(attention_output_rows, weight, preferred_element_type=jnp.float32)
    projection_output = projection_output + adapter_scale_factor * jnp.dot(
        bottleneck_activation, gathered_up_weight, preferred_element_type=jnp.float32
    )
    mixed_update = (projection_output * gate_row).astype(jnp.bfloat16)
    gated_branch_gradient = (cotangent.astype(jnp.float32) * gate_row).astype(jnp.bfloat16)
    bottleneck_gradient = (
        adapter_scale_factor
        * jnp.dot(gated_branch_gradient, gathered_up_weight.T, preferred_element_type=jnp.float32)
    ).astype(jnp.bfloat16)
    attention_output_gradient = jnp.dot(
        gated_branch_gradient, weight.T, preferred_element_type=jnp.float32
    )
    attention_output_gradient = (
        attention_output_gradient
        + jnp.dot(bottleneck_gradient, down_all.T, preferred_element_type=jnp.float32)
    ).astype(jnp.bfloat16)
    term_down = jnp.dot(
        attention_output_rows.T, bottleneck_gradient, preferred_element_type=jnp.float32
    )
    term_up = jnp.dot(
        bottleneck_activation.T, gated_branch_gradient, preferred_element_type=jnp.float32
    )
    gradient_scale_factor = (row_count * dp_count * fsdp_count) ** (-0.5)
    shard_terms = (
        lax.psum_scatter(term_down, "fsdp", scatter_dimension=0, tiled=True),
        lax.psum_scatter(term_up, "fsdp", scatter_dimension=1, tiled=True),
    )
    summed_down, reduced_up_gradient = lax.psum((shard_terms[0], shard_terms[1]), "dp")
    down_grad = summed_down * gradient_scale_factor
    scaled_up_gradient = reduced_up_gradient * (adapter_scale_factor * gradient_scale_factor)
    return (mixed_update, attention_output_gradient, down_grad, scaled_up_gradient)


def solution(mesh):
    in_specs = (
        P(("dp", "fsdp"), None),
        P(("dp", "fsdp"), None),
        P("fsdp", None),
        P("fsdp"),
        P("fsdp", None),
        P(None, "fsdp"),
        P("fsdp", None),
        P(),
    )
    out_specs = (P(("dp", "fsdp"), None), P(("dp", "fsdp"), None), P("fsdp", None), P(None, "fsdp"))
    return jax.shard_map(
        per_device, mesh=mesh, in_specs=in_specs, out_specs=out_specs, check_vma=False
    )
```

profile of v0, /device:TPU:0, one launch (start us, length us, event | category | flops | bytes accessed | tf_op | source)
XLA Modules:
  0.0 392.3 jit_solution(16552071789439468459)
XLA Ops:
  7.2 0.7 all-gather.5.cloned.1.call-update
  8.0 1.2 dynamic_slice.3
  10.0 1.7 copy.17
  11.7 35.1 %all_gather.18 = bf16[128,3072]{1,0:T(8,128)(2,1)S(1)} all-gather(bf16[128,384]{1,0:T(8,128)(2,1)S(1)} %copy-done.5), channel_id=1, replica_groups=mesh['dp'=4,'fsdp'=8] {'fsdp'}, dimensions={1}, use_global_device_ids=true | all-gather | bytes 884736 | tf_op jit(solution)/shard_map/all_gather | solution.py:38
  46.8 12.7 %all-gather.5.cloned.1.call-done = bf16[256,3072]{1,0:T(8,128)(2,1)} async-done(((bf16[32,3072]{1,0:T(8,128)(2,1)}), bf16[256,3072]{1,0:T(8,128)(2,1)}) %all-gather.5.cloned.1.call-update) | async-done | bytes 1572880 | tf_op jit(solution)/shard_map/all_gather | solution.py:39
  59.6 1.7 fusion.7
  61.3 1.1 fusion.5
  62.4 0.6 copy-done.3
  63.0 1.2 convolution_bitcast_fusion.1
  64.2 2.3 copy.21
  66.6 31.4 %all_gather.17 = bf16[1536,128]{1,0:T(8,128)(2,1)S(1)} all-gather(bf16[192,128]{1,0:T(8,128)(2,1)} %param.12), channel_id=1, replica_groups=mesh['dp'=4,'fsdp'=8] {'fsdp'}, dimensions={0}, use_global_device_ids=true | all-gather | bytes 442368 | tf_op jit(solution)/shard_map/all_gather | solution.py:37
  98.4 0.6 copy-done.1
  99.0 2.0 fusion.6
  101.1 27.4 %reduce-scatter.7.cloned.1.call-done = f32[192,128]{1,0:T(8,128)} async-done(((f32[1536,128]{1,0:T(8,128)}), f32[192,128]{1,0:T(8,128)}) %reduce-scatter.7.cloned.1.call-update) | async-done | bytes 98320
  128.5 1.6 copy.22
  130.1 66.5 %reduce-scatter.5.cloned.1.call-done = f32[128,384]{1,0:T(8,128)} async-done(((f32[128,3072]{1,0:T(8,128)}), f32[128,384]{1,0:T(8,128)}) %reduce-scatter.5.cloned.1.call-update) | async-done | bytes 196624 | tf_op jit(solution)/shard_map/reduce_scatter | solution.py:81
  196.8 0.5 all-gather.3.cloned.1.call-update
  198.0 0.6 dynamic-slice
  199.2 0.6 broadcast.20
  199.8 1.4 dynamic-update-slice
  201.3 19.6 %all-reduce = bf16[1536]{0:T(1024)(128)(2,1)S(1)} all-reduce(bf16[1536]{0:T(1024)(128)(2,1)} %dynamic-update-slice), channel_id=1, replica_groups=mesh['dp'=4,'fsdp'=8] {'fsdp'}, use_global_device_ids=true, to_apply=%add | all-reduce | flops 1536 | bytes 6144
  220.8 0.6 convert_element_type.35
  221.4 9.4 %all-reduce.4.cloned.1.call-done = (f32[192,128]{0,1:T(8,128)}, f32[128,384]{1,0:T(8,128)}) async-done(((f32[192,128]{0,1:T(8,128)}, f32[128,384]{1,0:T(8,128)}), (f32[192,128]{0,1:T(8,128)}, f32[128,384]{1,0:T(8,128)})) %all-reduce.4.cloned.1.call-update) | async-done | bytes 294928 | tf_op jit(solution)/shard_map/psum | solution.py:83
  230.9 1.6 broadcast_multiply_fusion.1
  232.4 1.6 copy.19
  234.1 1.6 broadcast_multiply_fusion
  235.7 135.3 %all-gather.3.cloned.1.call-done = bf16[1536,3072]{1,0:T(8,128)(2,1)} async-done(((bf16[192,3072]{1,0:T(8,128)(2,1)}), bf16[1536,3072]{1,0:T(8,128)(2,1)}) %all-gather.3.cloned.1.call-update) | async-done | bytes 9437200 | tf_op jit(solution)/shard_map/all_gather | solution.py:30
  371.0 7.2 %fusion.3 = f32[256,1536]{1,0:T(8,128)S(1)} fusion(bf16[1536,3072]{1,0:T(8,128)(2,1)} %all-gather.3.cloned.1.call-done, f32[1536]{0:T(1024)} %convert_element_type.35, bf16[256,3072]{0,1:T(8,128)(2,1)S(1)} %copy.17, f32[3072]{0:T(1024)S(1)} %bitcast.25), kind=kOutput, calls=%fused_computation.6 | convolution fusion | flops 2432434176 | bytes 12601344 | tf_op jit(solution)/shard_map/dot_general | solution.py:65
  378.2 1.2 fusion.4
  379.5 3.6 convolution_bitcast_fusion
  383.2 0.8 fusion.2
  384.0 1.7 copy.18
  (29 shorter events, 0.7 us)
Async XLA Ops:
  7.2 55.8 %copy-start = (bf16[256,1536]{1,0:T(8,128)(2,1)S(1)}, bf16[256,1536]{1,0:T(8,128)(2,1)}, u32[]{:S(2)}) copy-start(bf16[256,1536]{1,0:T(8,128)(2,1)} %param.8) | copy-start | bytes 2359300
  7.2 4.5 %copy-start.5 = (bf16[128,384]{1,0:T(8,128)(2,1)S(1)}, bf16[128,384]{1,0:T(8,128)(2,1)}, u32[]{:S(2)}) copy-start(bf16[128,384]{1,0:T(8,128)(2,1)} %param.13) | copy-start | bytes 294916
  7.2 52.4 %all-gather.5.cloned.1.call-start = ((), (), s32[]{:S(2)}) async-start(), calls=%async_computation.3 | async-start | bytes 1769472 | tf_op jit(solution)/shard_map/all_gather | solution.py:39
  7.9 120.6 %reduce-scatter.7.cloned.1.call-start = ((), (), s32[]{:S(2)}) async-start(), calls=%async_computation.5 | async-start | bytes 884736
  62.4 0.6 copy-start.3
  66.5 130.2 %reduce-scatter.5.cloned.1.call-start = ((), (), s32[]{:S(2)}) async-start(), calls=%async_computation.4 | async-start | bytes 1769472 | tf_op jit(solution)/shard_map/reduce_scatter | solution.py:81
  98.4 0.6 copy-start.1
  99.0 99.0 %copy-start.8 = (u32[32]{0:T(128)S(1)}, u32[32]{0:T(128)}, u32[]{:S(2)}) copy-start(u32[32]{0:T(128)} %constant.47) | copy-start | bytes 388
  101.0 129.8 %all-reduce.4.cloned.1.call-start = ((), (), s32[]{:S(2)}) async-start(), calls=%async_computation.6 | async-start | bytes 655360 | tf_op jit(solution)/shard_map/psum | solution.py:83
  196.7 174.3 %all-gather.3.cloned.1.call-start = ((), (), s32[]{:S(2)}) async-start(), calls=%async_computation.2 | async-start | bytes 10616832 | tf_op jit(solution)/shard_map/all_gather | solution.py:30
  371.0 7.2 %copy-start.4 = (bf16[256,128]{1,0:T(8,128)(2,1)S(1)}, bf16[256,128]{1,0:T(8,128)(2,1)}, u32[]{:S(2)}) copy-start(bf16[256,128]{1,0:T(8,128)(2,1)} %copy-done.3) | copy-start | bytes 196612
  371.0 8.5 %copy-start.6 = (f32[1536]{0:T(1024)S(1)}, f32[1536]{0:T(1024)}, u32[]{:S(2)}) copy-start(f32[1536]{0:T(1024)} %convert_element_type.35) | copy-start | bytes 18436
  371.0 8.5 %copy-start.7 = (bf16[1536,3072]{1,0:T(8,128)(2,1)S(1)}, bf16[1536,3072]{1,0:T(8,128)(2,1)}, u32[]{:S(2)}) copy-start(bf16[1536,3072]{1,0:T(8,128)(2,1)} %all-gather.3.cloned.1.call-done) | copy-start | bytes 28311556
  379.5 3.7 copy-start.2
Sparse Core Ops, SparseCore 0:
  10.2 49.2 all-gather.4
  66.6 61.8 reduce-scatter.6
  132.9 63.7 reduce-scatter.4
  199.5 31.3 all-reduce.3
  232.9 138.0 all-gather.2
where the time goes:
time: 393 us; the launch traced here: 392 us
  waiting for transfers between devices  253 us (64%)
  blocking collectives  86.2 us (22%)
  matrix products  19.3 us (5%)
  between operations  15.9 us (4%)
  local copies, waits for them, and re-layouts  14.2 us (4%)
    all_gather x1, waiting for transfers between devices, per_device(): lax.all_gather(quantized_weight_codes, 'fsdp', axis=0, tiled=True)  135 us
    reduce_scatter x1, waiting for transfers between devices, per_device(): lax.psum_scatter(term_up, 'fsdp', scatter_dimension=1, tiled=True)  66.5 us
    all_gather x1, blocking collectives, per_device(): lax.all_gather(adapter_up_weight, 'fsdp', axis=1, tiled=True)  35.1 us
    all_gather x1, blocking collectives, per_device(): lax.all_gather(adapter_down_weight, 'fsdp', axis=0, tiled=True)  31.4 us
    unnamed x6, waiting for transfers between devices  28.7 us
    unnamed x1, blocking collectives  19.6 us
    unnamed x27, local copies, waits for them, and re-layouts  12.9 us
    all_gather x1, waiting for transfers between devices, per_device(): lax.all_gather(timestep_gate_weight, 'fsdp', axis=0, tiled=True)  12.7 us
  transfers between devices with their start and end apart: 5, of which 5 were waited for; matrix products, arithmetic and copies ran while one was open for 4% of the time, Pallas kernels for 0%

commit v1 on v0

--- a/solution.py
+++ b/solution.py
@@ -1,8 +1,11 @@
+import functools
 import math
 
 import jax
 import jax.numpy as jnp
 from jax import lax
+from jax.experimental import pallas as pl
+from jax.experimental.pallas import tpu as pltpu
 from jax.sharding import PartitionSpec as P
 
 FREQ = 256
@@ -86,6 +89,417 @@
     return (mixed_update, attention_output_gradient, down_grad, scaled_up_gradient)
 
 
+MESH = pl.DeviceIdType.MESH
+ORDER = (1, 3, 2)
+NT = (((1,), (1,)), ((), ()))
+TN = (((0,), (0,)), ((), ()))
+
+
+def dot(a, b, dims=(((1,), (0,)), ((), ()))):
+    return lax.dot_general(a, b, dims, preferred_element_type=jnp.float32)
+
+
+class Place:
+    def __init__(self):
+        self.dp, self.f = lax.axis_index("dp"), lax.axis_index("fsdp")
+        self.c, self.x = lax.rem(self.dp, 2), lax.rem(lax.div(self.dp, 2), 2)
+        self.y, self.z = lax.rem(self.f, 2), lax.div(self.f, 2)
+
+    def far(self, k):
+        z = self.z
+        if k == 1:
+            return z + 1 - 2 * lax.rem(z, 2)
+        if k == 2:
+            return z + 2 - 4 * lax.div(z, 2)
+        return 3 - z
+
+    def device(self, way):
+        if way == "c":
+            return {"dp": self.dp + 1 - 2 * self.c, "fsdp": self.f}
+        if way == "x":
+            return {"dp": self.dp + 2 - 4 * self.x, "fsdp": self.f}
+        if way == "y":
+            return {"dp": self.dp, "fsdp": self.f + 1 - 2 * self.y}
+        return {"dp": self.dp, "fsdp": 2 * self.far(way) + self.y}
+
+
+class Post:
+    def __init__(self, place, send_sems, recv_sems):
+        self.place, self.ss, self.rs = place, send_sems, recv_sems
+        self.index, self.sent = {}, []
+
+    def _copy(self, name, way, src, dst):
+        i = self.index.setdefault(name, len(self.index))
+        return pltpu.make_async_remote_copy(
+            src_ref=src,
+            dst_ref=dst,
+            send_sem=self.ss.at[i],
+            recv_sem=self.rs.at[i],
+            device_id=self.place.device(way),
+            device_id_type=MESH,
+        )
+
+    def send(self, name, way, src, dst=None):
+        copy = self._copy(name, way, src, src if dst is None else dst)
+        copy.start()
+        self.sent.append(copy)
+
+    def wait(self, name, way, dst):
+        self._copy(name, way, dst, dst).wait_recv()
+
+    def finish(self):
+        for copy in self.sent:
+            copy.wait_send()
+
+
+class Gather:
+    def __init__(self, tag, post, place, piece):
+        self.tag, self.post, self.p, self.piece = tag, post, place, piece
+
+    def send(self, name, way, region):
+        self.post.send((self.tag, name), way, region)
+
+    def wait(self, name, way, region):
+        self.post.wait((self.tag, name), way, region)
+
+    def start(self):
+        p = self.p
+        own = self.piece(p.c, p.x, p.z, p.y)
+        self.send("oy", "y", own)
+        for k in ORDER:
+            self.send(("z", k), k, own)
+
+    def own_first(self):
+        p = self.p
+        got = self.piece(p.c, p.x, p.z, 1 - p.y)
+        self.wait("oy", "y", got)
+        self.send("ox", "x", got)
+        self.send("oc1", "c", got)
+
+    def own_second(self):
+        p = self.p
+        got = self.piece(p.c, 1 - p.x, p.z, 1 - p.y)
+        self.wait("ox", "x", got)
+        self.send("oc2", "c", got)
+
+    def own_end(self):
+        p = self.p
+        self.wait("oc1", "c", self.piece(1 - p.c, p.x, p.z, 1 - p.y))
+        self.wait("oc2", "c", self.piece(1 - p.c, 1 - p.x, p.z, 1 - p.y))
+
+    def first(self, k):
+        p = self.p
+        got = self.piece(p.c, p.x, p.far(k), p.y)
+        self.wait(("z", k), k, got)
+        self.send(("x", k), "x", got)
+        self.send(("y", k), "y", got)
+        self.send(("c1", k), "c", got)
+
+    def second(self, k):
+        p = self.p
+        zz = p.far(k)
+        got = self.piece(p.c, p.x, zz, 1 - p.y)
+        self.wait(("y", k), "y", got)
+        self.send(("xh", k), "x", self.piece(p.c, p.x, zz, 1 - p.y, "u"))
+        self.send(("c3", k), "c", got)
+        got = self.piece(p.c, 1 - p.x, zz, p.y)
+        self.wait(("x", k), "x", got)
+        self.send(("yh", k), "y", self.piece(p.c, 1 - p.x, zz, p.y, "l"))
+        self.send(("c2", k), "c", got)
+
+    def third(self, k):
+        p = self.p
+        zz = p.far(k)
+        for name, way, part in (("xh", "x", "u"), ("yh", "y", "l")):
+            got = self.piece(p.c, 1 - p.x, zz, 1 - p.y, part)
+            self.wait((name, k), way, got)
+            self.send(("d" + part, k), "c", got)
+
+    def end(self, k):
+        p = self.p
+        zz, c = p.far(k), 1 - p.c
+        self.wait(("c1", k), "c", self.piece(c, p.x, zz, p.y))
+        self.wait(("c3", k), "c", self.piece(c, p.x, zz, 1 - p.y))
+        self.wait(("c2", k), "c", self.piece(c, 1 - p.x, zz, p.y))
+        for part in "ul":
+            self.wait(("d" + part, k), "c", self.piece(c, 1 - p.x, zz, 1 - p.y, part))
+
+
+MESSAGES = 2 * (10 * len(ORDER) + 4) + 4 + 7
+
+
+def kernel(
+    scales,
+    x_hbm, cot_hbm, codes, amax, down, up, gate, feat,
+    mixed_hbm, aog_hbm, dn_out, up_out,
+    w, pre, x, cot, bg, acc, mixed, aog, bacc, upf, downf, lr, bn, grow,
+    gates, gf, g_send, g_got, g_sum, z_send, z_got, y_send, y_got, half, half_got, whole,
+    send_sems, recv_sems, local_sems,
+):
+    place = Place()
+    post = Post(place, send_sems, recv_sems)
+    rows, width = codes.shape
+    quarter = width // 4
+    shard_up = up.shape[1]
+    rank = up.shape[0]
+    part = down.shape[0] // 3
+
+    load_x = pltpu.make_async_copy(x_hbm, x, local_sems.at[0])
+    load_x.start()
+    load_cot = pltpu.make_async_copy(cot_hbm, cot, local_sems.at[1])
+    load_cot.start()
+
+    barrier = pltpu.get_barrier_semaphore()
+    ways = ("c", "x", "y") + ORDER
+    for way in ways:
+        pl.semaphore_signal(barrier, inc=1, device_id=place.device(way), device_id_type=MESH)
+
+    def w_piece(c, xx, zz, yy, which=""):
+        start, size = {"": (0, rows), "l": (0, rows // 2), "u": (rows // 2, rows // 2)}[which]
+        begin = pl.multiple_of((2 * zz + yy) * rows + start, rows // 2)
+        return w.at[2 * c + xx, pl.ds(begin, size)]
+
+    def pre_piece(c, xx, zz, yy, which=""):
+        start, size = {"": (0, 48), "l": (0, 32), "u": (32, 16)}[which]
+        begin = pl.multiple_of((2 * c + xx) * 48 + start, 16)
+        return pre.at[2 * zz + yy, pl.ds(begin, size)]
+
+    big = Gather("w", post, place, w_piece)
+    small = Gather("p", post, place, pre_piece)
+    own = pl.ds(pl.multiple_of(place.f * rows, rows), rows)
+    factor = amax[...].astype(jnp.float32)
+
+    pre[place.f, :rank, :] = up[...]
+    for j in range(3):
+        pre[place.f, rank:, j * 128 : (j + 1) * 128] = down[j * part : (j + 1) * part, :]
+    gates[0] = dot(feat[...], gate[...])[0:1]
+
+    def scale(q):
+        columns = pl.ds(pl.multiple_of(q * quarter, 128), quarter)
+        w[q, own, :] = (codes[:, columns].astype(jnp.float32) * factor).astype(jnp.bfloat16)
+
+    mine = 2 * place.c + place.x
+    scale(mine)
+    pl.semaphore_wait(barrier, len(ways))
+
+    post.send("gy", "y", gates.at[0], gates.at[1])
+    small.start()
+    big.start()
+    for i in range(1, 4):
+        scale(lax.rem(mine + i, 4))
+
+    post.wait("gy", "y", gates.at[1])
+    gates[2] = gates[0] + gates[1]
+    for i, k in enumerate(ORDER):
+        post.send(("gz", k), k, gates.at[2], gates.at[3 + i])
+    small.own_first()
+    for k in ORDER:
+        small.first(k)
+    small.own_second()
+    for k in ORDER:
+        small.second(k)
+    for i, k in enumerate(ORDER):
+        post.wait(("gz", k), k, gates.at[3 + i])
+    grow[...] = gates[2] + gates[3] + gates[4] + gates[5]
+    for k in ORDER:
+        small.third(k)
+    big.own_first()
+    big.first(ORDER[0])
+    small.own_end()
+    for k in ORDER:
+        small.end(k)
+
+    @pl.loop(0, 8)
+    def _(f):
+        upf[:, pl.ds(pl.multiple_of(f * shard_up, 128), shard_up)] = pre[f, :rank, :]
+        for j in range(3):
+            to = pl.ds(pl.multiple_of(f * rows + j * part, part), part)
+            downf[to, :] = pre[f, rank:, j * 128 : (j + 1) * 128]
+
+    load_x.wait()
+    load_cot.wait()
+    lr[...] = dot(x[...], downf[...]).astype(jnp.bfloat16)
+    bacc[:, :rank] = jnp.zeros((x.shape[0], rank), jnp.float32)
+
+    @pl.loop(0, 4)
+    def _(q):
+        columns = pl.ds(pl.multiple_of(q * quarter, 128), quarter)
+        branch = (cot[:, columns].astype(jnp.float32) * grow[:, columns]).astype(jnp.bfloat16)
+        bg[q] = branch
+        ups = upf[:, columns]
+        bacc[:, :rank] += dot(branch, ups, NT)
+        acc[q] = 0.5 * dot(lr[...], ups)
+        term = dot(lr[...], branch, TN)
+        gf[2 * q, :rank, :] = term[:, :shard_up]
+        gf[2 * q + 1, :rank, :] = term[:, shard_up:]
+
+    bn[...] = (0.5 * bacc[:, :rank]).astype(jnp.bfloat16)
+
+    @pl.loop(0, 4)
+    def _(zz):
+        columns = pl.ds(pl.multiple_of(zz * 2 * rows, 128), 2 * rows)
+        term = dot(x[:, columns], bn[...], TN)
+        for b in range(6):
+            gf[2 * zz + b // 3, rank:, (b % 3) * 128 : (b % 3 + 1) * 128] = term[b * part : (b + 1) * part]
+
+    hrows = rows // 2
+    keep = pl.ds(pl.multiple_of(place.c * hrows, hrows), hrows)
+    give = pl.ds(pl.multiple_of((1 - place.c) * hrows, hrows), hrows)
+    g_send[...] = gf[:, give, :].astype(jnp.bfloat16)
+    post.send("rc", "c", g_send, g_got)
+
+    big.own_second()
+    big.first(ORDER[1])
+    big.second(ORDER[0])
+
+    post.wait("rc", "c", g_got)
+    g_sum[...] = gf[:, keep, :] + g_got[...].astype(jnp.float32)
+    z_send[...] = g_sum[...].astype(jnp.bfloat16)
+    for i, k in enumerate(ORDER):
+        post.send(("rz", k), k, z_send.at[pl.ds(2 * place.far(k), 2)], z_got.at[i])
+
+    stores = []
+
+    def plane(zz):
+        at = pl.ds(pl.multiple_of(zz * 2 * rows, 128), 2 * rows)
+        bacc[...] = dot(bn[...], downf[at, :], NT)
+
+        @pl.loop(0, 4)
+        def _(q):
+            block = w[q, at, :]
+            acc[q] += dot(x[:, at], block)
+            bacc[...] += dot(bg[q], block, NT)
+
+        aog[:, at] = bacc[...].astype(jnp.bfloat16)
+        store = pltpu.make_async_copy(aog.at[:, at], aog_hbm.at[:, at], local_sems.at[2 + len(stores)])
+        store.start()
+        stores.append(store)
+
+    big.own_end()
+    plane(place.z)
+    big.third(ORDER[0])
+    big.first(ORDER[2])
+    big.second(ORDER[1])
+
+    total = g_sum[pl.ds(2 * place.z, 2)]
+    for i, k in enumerate(ORDER):
+        post.wait(("rz", k), k, z_got.at[i])
+        total = total + z_got[i].astype(jnp.float32)
+    g_sum[pl.ds(2 * place.z, 2)] = total
+    y_send[...] = g_sum[2 * place.z + 1 - place.y].astype(jnp.bfloat16)
+    post.send("ry", "y", y_send, y_got)
+
+    big.end(ORDER[0])
+    plane(place.far(ORDER[0]))
+    big.third(ORDER[1])
+    big.second(ORDER[2])
+
+    post.wait("ry", "y", y_got)
+    half[...] = g_sum[place.f] + y_got[...].astype(jnp.float32)
+    post.send("rx", "x", half, half_got)
+
+    big.end(ORDER[1])
+    plane(place.far(ORDER[1]))
+
+    post.wait("rx", "x", half_got)
+    whole[place.c] = half[...] + half_got[...]
+    post.send("rd", "c", whole.at[place.c])
+
+    big.third(ORDER[2])
+    post.wait("rd", "c", whole.at[1 - place.c])
+    for i in range(rank // 32):
+        r = i * 32
+        up_out[r : r + 32, :] = whole[r // hrows, r % hrows : r % hrows + 32, :] * scales[1]
+    for j in range(3):
+        dn_out[j * part : (j + 1) * part, :] = (
+            whole[1, rank - hrows :, j * 128 : (j + 1) * 128] * scales[0]
+        )
+
+    big.end(ORDER[2])
+    plane(place.far(ORDER[2]))
+    for q in range(4):
+        at = pl.ds(q * quarter, quarter)
+        mixed[:, at] = (acc[q] * grow[:, at]).astype(jnp.bfloat16)
+        store = pltpu.make_async_copy(mixed.at[:, at], mixed_hbm.at[:, at], local_sems.at[2 + len(stores)])
+        store.start()
+        stores.append(store)
+    post.finish()
+    for store in stores:
+        store.wait()
+
+
+def fused(x, cot, codes, amax, down, up, gate, timesteps):
+    tokens, inner = x.shape
+    width, rank = cot.shape[1], up.shape[0]
+    rows = codes.shape[0]
+    dp_count, fsdp_count = lax.axis_size("dp"), lax.axis_size("fsdp")
+    per = gate.shape[0]
+    sample = (lax.axis_index("dp") * fsdp_count) * tokens // PATCHES
+    step = lax.dynamic_slice_in_dim(timesteps, sample, 1).astype(jnp.float32)
+    number = lax.axis_index("fsdp") * per + jnp.arange(per, dtype=jnp.int32)
+    half_freq = FREQ // 2
+    frequency = jnp.exp(
+        -math.log(10000.0) * (number % half_freq).astype(jnp.float32) / half_freq
+    )
+    angle = step * frequency
+    feat = jnp.where(number < half_freq, jnp.cos(angle), jnp.sin(angle)).astype(jnp.bfloat16)
+    feat = jnp.broadcast_to(feat[None, :], (16, per))
+    gradient_scale = (tokens * dp_count * fsdp_count) ** (-0.5)
+    bf, f32 = jnp.bfloat16, jnp.float32
+    quarter, hrows = width // 4, rows // 2
+    vmem = pl.BlockSpec(memory_space=pltpu.VMEM)
+    hbm = pl.BlockSpec(memory_space=pl.ANY)
+    return pl.pallas_call(
+        functools.partial(kernel, (gradient_scale, adapter_scale_factor * gradient_scale)),
+        out_shape=(
+            jax.ShapeDtypeStruct((tokens, width), bf),
+            jax.ShapeDtypeStruct((tokens, inner), bf),
+            jax.ShapeDtypeStruct((rows, rank), f32),
+            jax.ShapeDtypeStruct((rank, up.shape[1]), f32),
+        ),
+        in_specs=[hbm, hbm] + [vmem] * 6,
+        out_specs=(hbm, hbm, vmem, vmem),
+        scratch_shapes=[
+            pltpu.VMEM((4, inner, quarter), bf),
+            pltpu.VMEM((8, rows, up.shape[1]), bf),
+            pltpu.VMEM((tokens, inner), bf),
+            pltpu.VMEM((tokens, width), bf),
+            pltpu.VMEM((4, tokens, quarter), bf),
+            pltpu.VMEM((4, tokens, quarter), f32),
+            pltpu.VMEM((tokens, width), bf),
+            pltpu.VMEM((tokens, inner), bf),
+            pltpu.VMEM((tokens, 2 * rows), f32),
+            pltpu.VMEM((rank, width), bf),
+            pltpu.VMEM((inner, rank), bf),
+            pltpu.VMEM((tokens, rank), bf),
+            pltpu.VMEM((tokens, rank), bf),
+            pltpu.VMEM((1, width), f32),
+            pltpu.VMEM((6, 1, width), f32),
+            pltpu.VMEM((8, rows, up.shape[1]), f32),
+            pltpu.VMEM((8, hrows, up.shape[1]), bf),
+            pltpu.VMEM((8, hrows, up.shape[1]), bf),
+            pltpu.VMEM((8, hrows, up.shape[1]), f32),
+            pltpu.VMEM((8, hrows, up.shape[1]), bf),
+            pltpu.VMEM((3, 2, hrows, up.shape[1]), bf),
+            pltpu.VMEM((hrows, up.shape[1]), bf),
+            pltpu.VMEM((hrows, up.shape[1]), bf),
+            pltpu.VMEM((hrows, up.shape[1]), f32),
+            pltpu.VMEM((hrows, up.shape[1]), f32),
+            pltpu.VMEM((2, hrows, up.shape[1]), f32),
+            pltpu.SemaphoreType.DMA((MESSAGES,)),
+            pltpu.SemaphoreType.DMA((MESSAGES,)),
+            pltpu.SemaphoreType.DMA((10,)),
+        ],
+        compiler_params=pltpu.CompilerParams(
+            collective_id=0, has_side_effects=True, vmem_limit_bytes=56 * 1024 * 1024
+        ),
+    )(x, cot, codes, amax[None, :], down, up, gate, feat)
+
+
+def fits(mesh):
+    return mesh.shape["dp"] == 4 and mesh.shape["fsdp"] == 8
+
+
 def solution(mesh):
     in_specs = (
         P(("dp", "fsdp"), None),
@@ -99,5 +513,5 @@
     )
     out_specs = (P(("dp", "fsdp"), None), P(("dp", "fsdp"), None), P("fsdp", None), P(None, "fsdp"))
     return jax.shard_map(
-        per_device, mesh=mesh, in_specs=in_specs, out_specs=out_specs, check_vma=False
-    )
+        fused if fits(mesh) else per_device, mesh=mesh, in_specs=in_specs, out_specs=out_specs, check_vma=False
+    )

time: 393 us -> 93.8 us (0.24)
  waiting for transfers between devices: 253 us -> 0 us
  blocking collectives: 86.2 us -> 0 us
  Pallas kernels: 0 us -> 84.2 us
  matrix products: 19.3 us -> 0 us
  between operations: 15.9 us -> 1.98 us
  local copies, waits for them, and re-layouts: 14.2 us -> 6.85 us
    all_gather x2 -> x0, waiting for transfers between devices: 148 us -> none  [the longest x1 135 us: per_device(): lax.all_gather(quantized_weight_codes, 'fsdp', axis=0, tiled=True)]
    pallas_call x0 -> x1, Pallas kernels: none -> 84.2 us  [fused(): pl.pallas_call(functools.partial(kernel, (gradient_scale, adapter_scale_f...]
    all_gather x2 -> x0, blocking collectives: 66.6 us -> none  [the longest x1 35.1 us: per_device(): lax.all_gather(adapter_up_weight, 'fsdp', axis=1, tiled=True)]
    reduce_scatter x1 -> x0, waiting for transfers between devices: 66.5 us -> none  [per_device(): lax.psum_scatter(term_up, 'fsdp', scatter_dimension=1, tiled=True)]
    unnamed x6 -> x0, waiting for transfers between devices: 28.7 us -> none
    unnamed x1 -> x0, blocking collectives: 19.6 us -> none
    dot_general x9 -> x0, matrix products: 19.3 us -> none  [the longest x1 7.2 us: per_device(): jnp.dot(gated_branch_gradient, weight.T, preferred_element_type=jnp.float32)]
    psum x1 -> x0, waiting for transfers between devices: 9.42 us -> none  [per_device(): lax.psum((shard_terms[0], shard_terms[1]), 'dp')]
  transfers between devices with their start and end apart: 5 -> 0, of which waited for: 5 -> 0; matrix products, arithmetic and copies ran while one was open for 4% -> 0% of each run, Pallas kernels for 0% -> 0%
where the time goes in v1:
time: 93.8 us; the launch traced here: 93.1 us
  Pallas kernels  84.2 us (90%)
  local copies, waits for them, and re-layouts  6.85 us (7%)
  between operations  1.98 us (2%)
    pallas_call x1, Pallas kernels, fused(): pl.pallas_call(functools.partial(kernel, (gradient_scale, adapter_scale_f...  84.2 us
    unnamed x10, local copies, waits for them, and re-layouts  5.01 us

profile of v1, /device:TPU:0, one launch (start us, length us, event | category | flops | bytes accessed | tf_op | source)
XLA Modules:
  0.0 93.1 jit_solution(4784228395120238211)
XLA Ops:
  1.3 1.2 %dynamic_slice.3 = s32[1]{0:T(128)} dynamic-slice(s32[2]{0:T(128)} %param.15, s32[]{:T(128)S(6)} %select_n.27), dynamic_slice_sizes={1} | dynamic-slice | bytes 12 | tf_op jit(solution)/shard_map/dynamic_slice | solution.py:438
  3.2 0.1 fusion
  3.3 0.6 broadcast_in_dim.10.feat
  3.9 84.2 %shard_map.111 = (bf16[256,3072]{1,0:T(8,128)(2,1)}, bf16[256,1536]{1,0:T(8,128)(2,1)}, f32[192,128]{1,0:T(8,128)}, f32[128,384]{1,0:T(8,128)}) custom-call(bf16[256,1536]{1,0:T(8,128)(2,1)} %x_hbm.1, bf16[256,3072]{1,0:T(8,128)(2,1)} %cot_hbm.1, bf16[192,3072]{1,0:T(8,128)(2,1)} %codes.1, bf16[1,1]{1,0:T(2,128)(2,1)} %bitcast.2.amax, ...), custom_call_target="tpu_custom_call" | custom-call | tf_op jit(solution)/shard_map/pallas_call | solution.py:452
  88.1 0.0 copy-start
  88.1 2.7 %copy.17 = bf16[256,3072]{1,0:T(8,128)(2,1)} copy(bf16[256,3072]{1,0:T(8,128)(2,1)} %get-tuple-element.8) | data formatting | bytes 3145728
  90.8 0.0 copy-done
  90.8 0.0 copy-start.2
  90.8 0.0 copy-start.1
  90.8 0.9 copy.18
  91.7 0.1 copy-done.2
  91.8 0.6 copy.19
  92.4 0.0 copy-done.1
  92.4 0.7 copy.20
Async XLA Ops:
  88.1 2.7 %copy-start = (bf16[256,1536]{1,0:T(8,128)(2,1)S(1)}, bf16[256,1536]{1,0:T(8,128)(2,1)}, u32[]{:S(2)}) copy-start(bf16[256,1536]{1,0:T(8,128)(2,1)} %get-tuple-element.9) | copy-start | bytes 2359300
  90.8 1.0 %copy-start.2 = (f32[192,128]{1,0:T(8,128)S(1)}, f32[192,128]{1,0:T(8,128)}, u32[]{:S(2)}) copy-start(f32[192,128]{1,0:T(8,128)} %get-tuple-element.10) | copy-start | bytes 294916
  90.8 1.6 %copy-start.1 = (f32[128,384]{1,0:T(8,128)S(1)}, f32[128,384]{1,0:T(8,128)}, u32[]{:S(2)}) copy-start(f32[128,384]{1,0:T(8,128)} %get-tuple-element.11) | copy-start | bytes 589828

commit v2 on v1

--- a/solution.py
+++ b/solution.py
@@ -162,77 +162,86 @@
     def wait(self, name, way, region):
         self.post.wait((self.tag, name), way, region)
 
-    def start(self):
-        p = self.p
-        own = self.piece(p.c, p.x, p.z, p.y)
-        self.send("oy", "y", own)
-        for k in ORDER:
-            self.send(("z", k), k, own)
-
-    def own_first(self):
-        p = self.p
-        got = self.piece(p.c, p.x, p.z, 1 - p.y)
-        self.wait("oy", "y", got)
-        self.send("ox", "x", got)
-        self.send("oc1", "c", got)
-
-    def own_second(self):
-        p = self.p
-        got = self.piece(p.c, 1 - p.x, p.z, 1 - p.y)
-        self.wait("ox", "x", got)
-        self.send("oc2", "c", got)
-
-    def own_end(self):
-        p = self.p
-        self.wait("oc1", "c", self.piece(1 - p.c, p.x, p.z, 1 - p.y))
-        self.wait("oc2", "c", self.piece(1 - p.c, 1 - p.x, p.z, 1 - p.y))
-
-    def first(self, k):
-        p = self.p
-        got = self.piece(p.c, p.x, p.far(k), p.y)
-        self.wait(("z", k), k, got)
-        self.send(("x", k), "x", got)
-        self.send(("y", k), "y", got)
-        self.send(("c1", k), "c", got)
-
-    def second(self, k):
+    def start_own(self):
+        p = self.p
+        for h in "lu":
+            self.send(("oy", h), "y", self.piece(p.c, p.x, p.z, p.y, h))
+
+    def start(self, k):
+        p = self.p
+        for h in "lu":
+            self.send(("z", k, h), k, self.piece(p.c, p.x, p.z, p.y, h))
+
+    def own_first(self, h):
+        p = self.p
+        got = self.piece(p.c, p.x, p.z, 1 - p.y, h)
+        self.wait(("oy", h), "y", got)
+        self.send(("ox", h), "x", got)
+        self.send(("oc1", h), "c", got)
+
+    def own_second(self, h):
+        p = self.p
+        got = self.piece(p.c, 1 - p.x, p.z, 1 - p.y, h)
+        self.wait(("ox", h), "x", got)
+        self.send(("oc2", h), "c", got)
+
+    def own_end(self, same):
+        p = self.p
+        for h in "lu":
+            if same:
+                self.wait(("oc1", h), "c", self.piece(1 - p.c, p.x, p.z, 1 - p.y, h))
+            else:
+                self.wait(("oc2", h), "c", self.piece(1 - p.c, 1 - p.x, p.z, 1 - p.y, h))
+
+    def first(self, k, h):
+        p = self.p
+        got = self.piece(p.c, p.x, p.far(k), p.y, h)
+        self.wait(("z", k, h), k, got)
+        self.send(("x", k, h), "x", got)
+        self.send(("y", k, h), "y", got)
+        self.send(("c1", k, h), "c", got)
+
+    def second(self, k, h):
         p = self.p
         zz = p.far(k)
-        got = self.piece(p.c, p.x, zz, 1 - p.y)
-        self.wait(("y", k), "y", got)
-        self.send(("xh", k), "x", self.piece(p.c, p.x, zz, 1 - p.y, "u"))
-        self.send(("c3", k), "c", got)
-        got = self.piece(p.c, 1 - p.x, zz, p.y)
-        self.wait(("x", k), "x", got)
-        self.send(("yh", k), "y", self.piece(p.c, 1 - p.x, zz, p.y, "l"))
-        self.send(("c2", k), "c", got)
+        got = self.piece(p.c, p.x, zz, 1 - p.y, h)
+        self.wait(("y", k, h), "y", got)
+        if h == "u":
+            self.send(("d", k, h), "x", got)
+        self.send(("c3", k, h), "c", got)
+        got = self.piece(p.c, 1 - p.x, zz, p.y, h)
+        self.wait(("x", k, h), "x", got)
+        if h == "l":
+            self.send(("d", k, h), "y", got)
+        self.send(("c2", k, h), "c", got)
 
     def third(self, k):
         p = self.p
-        zz = p.far(k)
-        for name, way, part in (("xh", "x", "u"), ("yh", "y", "l")):
-            got = self.piece(p.c, 1 - p.x, zz, 1 - p.y, part)
-            self.wait((name, k), way, got)
-            self.send(("d" + part, k), "c", got)
-
-    def end(self, k):
+        for h in "lu":
+            got = self.piece(p.c, 1 - p.x, p.far(k), 1 - p.y, h)
+            self.wait(("d", k, h), "y" if h == "l" else "x", got)
+            self.send(("c4", k, h), "c", got)
+
+    def end(self, k, same):
         p = self.p
         zz, c = p.far(k), 1 - p.c
-        self.wait(("c1", k), "c", self.piece(c, p.x, zz, p.y))
-        self.wait(("c3", k), "c", self.piece(c, p.x, zz, 1 - p.y))
-        self.wait(("c2", k), "c", self.piece(c, 1 - p.x, zz, p.y))
-        for part in "ul":
-            self.wait(("d" + part, k), "c", self.piece(c, 1 - p.x, zz, 1 - p.y, part))
-
-
-MESSAGES = 2 * (10 * len(ORDER) + 4) + 4 + 7
+        for h in "lu":
+            if same:
+                self.wait(("c1", k, h), "c", self.piece(c, p.x, zz, p.y, h))
+                self.wait(("c3", k, h), "c", self.piece(c, p.x, zz, 1 - p.y, h))
+            else:
+                self.wait(("c2", k, h), "c", self.piece(c, 1 - p.x, zz, p.y, h))
+                self.wait(("c4", k, h), "c", self.piece(c, 1 - p.x, zz, 1 - p.y, h))
+
+
+MESSAGES = 2 * (16 * len(ORDER) + 8) + 4 + 7
 
 
 def kernel(
     scales,
     x_hbm, cot_hbm, codes, amax, down, up, gate, feat,
     mixed_hbm, aog_hbm, dn_out, up_out,
-    w, pre, x, cot, bg, acc, mixed, aog, bacc, upf, downf, lr, bn, grow,
+    w, pre, x, cot, bg, acc, mixed, aog, bacc, bsum, upf, downf, lr, bn, grow,
     gates, gf, g_send, g_got, g_sum, z_send, z_got, y_send, y_got, half, half_got, whole,
     send_sems, recv_sems, local_sems,
 ):
@@ -254,13 +263,13 @@
     for way in ways:
         pl.semaphore_signal(barrier, inc=1, device_id=place.device(way), device_id_type=MESH)
 
-    def w_piece(c, xx, zz, yy, which=""):
-        start, size = {"": (0, rows), "l": (0, rows // 2), "u": (rows // 2, rows // 2)}[which]
+    def w_piece(c, xx, zz, yy, which):
+        start, size = {"l": (0, rows // 2), "u": (rows // 2, rows // 2)}[which]
         begin = pl.multiple_of((2 * zz + yy) * rows + start, rows // 2)
         return w.at[2 * c + xx, pl.ds(begin, size)]
 
-    def pre_piece(c, xx, zz, yy, which=""):
-        start, size = {"": (0, 48), "l": (0, 32), "u": (32, 16)}[which]
+    def pre_piece(c, xx, zz, yy, which):
+        start, size = {"l": (0, 32), "u": (32, 16)}[which]
         begin = pl.multiple_of((2 * c + xx) * 48 + start, 16)
         return pre.at[2 * zz + yy, pl.ds(begin, size)]
 
@@ -283,8 +292,12 @@
     pl.semaphore_wait(barrier, len(ways))
 
     post.send("gy", "y", gates.at[0], gates.at[1])
-    small.start()
-    big.start()
+    small.start_own()
+    for k in ORDER:
+        small.start(k)
+    big.start(1)
+    big.start_own()
+    big.start(3)
     for i in range(1, 4):
         scale(lax.rem(mine + i, 4))
 
@@ -292,22 +305,27 @@
     gates[2] = gates[0] + gates[1]
     for i, k in enumerate(ORDER):
         post.send(("gz", k), k, gates.at[2], gates.at[3 + i])
-    small.own_first()
+    for h in "lu":
+        small.own_first(h)
     for k in ORDER:
-        small.first(k)
-    small.own_second()
+        for h in "lu":
+            small.first(k, h)
+    big.own_first("l")
+    for h in "lu":
+        small.own_second(h)
     for k in ORDER:
-        small.second(k)
+        for h in "lu":
+            small.second(k, h)
+    big.own_first("u")
+    for k in ORDER:
+        small.third(k)
     for i, k in enumerate(ORDER):
         post.wait(("gz", k), k, gates.at[3 + i])
     grow[...] = gates[2] + gates[3] + gates[4] + gates[5]
-    for k in ORDER:
-        small.third(k)
-    big.own_first()
-    big.first(ORDER[0])
-    small.own_end()
-    for k in ORDER:
-        small.end(k)
+    for same in (True, False):
+        small.own_end(same)
+        for k in ORDER:
+            small.end(k, same)
 
     @pl.loop(0, 8)
     def _(f):
@@ -318,22 +336,31 @@
 
     load_x.wait()
     load_cot.wait()
+    big.first(1, "l")
     lr[...] = dot(x[...], downf[...]).astype(jnp.bfloat16)
-    bacc[:, :rank] = jnp.zeros((x.shape[0], rank), jnp.float32)
-
-    @pl.loop(0, 4)
-    def _(q):
-        columns = pl.ds(pl.multiple_of(q * quarter, 128), quarter)
-        branch = (cot[:, columns].astype(jnp.float32) * grow[:, columns]).astype(jnp.bfloat16)
-        bg[q] = branch
-        ups = upf[:, columns]
-        bacc[:, :rank] += dot(branch, ups, NT)
-        acc[q] = 0.5 * dot(lr[...], ups)
-        term = dot(lr[...], branch, TN)
-        gf[2 * q, :rank, :] = term[:, :shard_up]
-        gf[2 * q + 1, :rank, :] = term[:, shard_up:]
-
-    bn[...] = (0.5 * bacc[:, :rank]).astype(jnp.bfloat16)
+    bsum[...] = jnp.zeros_like(bsum)
+    big.first(1, "u")
+    big.start(2)
+
+    def adapter(begin, end):
+        @pl.loop(begin, end)
+        def _(q):
+            columns = pl.ds(pl.multiple_of(q * quarter, 128), quarter)
+            branch = (cot[:, columns].astype(jnp.float32) * grow[:, columns]).astype(jnp.bfloat16)
+            bg[q] = branch
+            ups = upf[:, columns]
+            bsum[...] += dot(branch, ups, NT)
+            acc[q] = 0.5 * dot(lr[...], ups)
+            term = dot(lr[...], branch, TN)
+            gf[2 * q, :rank, :] = term[:, :shard_up]
+            gf[2 * q + 1, :rank, :] = term[:, shard_up:]
+
+    adapter(0, 2)
+    big.own_second("l")
+    big.own_second("u")
+    adapter(2, 4)
+    big.second(1, "l")
+    bn[...] = (0.5 * bsum[...]).astype(jnp.bfloat16)
 
     @pl.loop(0, 4)
     def _(zz):
@@ -348,9 +375,49 @@
     g_send[...] = gf[:, give, :].astype(jnp.bfloat16)
     post.send("rc", "c", g_send, g_got)
 
-    big.own_second()
-    big.first(ORDER[1])
-    big.second(ORDER[0])
+    stores = []
+
+    def keep_store(source, target):
+        store = pltpu.make_async_copy(source, target, local_sems.at[2 + len(stores)])
+        store.start()
+        stores.append(store)
+
+    done = [0, 0, 0, 0]
+    quarters = {
+        "a": 2 * place.c + place.x,
+        "b": 2 * place.c + 1 - place.x,
+        "d": 2 - 2 * place.c + place.x,
+        "e": 2 - 2 * place.c + 1 - place.x,
+    }
+
+    def unit(k, which, last=False):
+        zz = place.far(k) if k else place.z
+        q = quarters[which]
+        at = pl.ds(pl.multiple_of(zz * 2 * rows, 128), 2 * rows)
+        block = w[q, at, :]
+        back = dot(bg[q], block, NT)
+        if done[k] == 0:
+            bacc[k] = back + dot(bn[...], downf[at, :], NT)
+        elif done[k] < 3:
+            bacc[k] += back
+        else:
+            aog[:, at] = (bacc[k] + back).astype(jnp.bfloat16)
+            keep_store(aog.at[:, at], aog_hbm.at[:, at])
+        done[k] += 1
+        total = acc[q] + dot(x[:, at], block)
+        if last:
+            columns = pl.ds(pl.multiple_of(q * quarter, 128), quarter)
+            mixed[:, columns] = (total * grow[:, columns]).astype(jnp.bfloat16)
+            keep_store(mixed.at[:, columns], mixed_hbm.at[:, columns])
+        else:
+            acc[q] = total
+
+    big.first(3, "l")
+    big.first(3, "u")
+    big.second(1, "u")
+    unit(0, "a")
+    unit(0, "b")
+    big.third(1)
 
     post.wait("rc", "c", g_got)
     g_sum[...] = gf[:, keep, :] + g_got[...].astype(jnp.float32)
@@ -358,28 +425,18 @@
     for i, k in enumerate(ORDER):
         post.send(("rz", k), k, z_send.at[pl.ds(2 * place.far(k), 2)], z_got.at[i])
 
-    stores = []
-
-    def plane(zz):
-        at = pl.ds(pl.multiple_of(zz * 2 * rows, 128), 2 * rows)
-        bacc[...] = dot(bn[...], downf[at, :], NT)
-
-        @pl.loop(0, 4)
-        def _(q):
-            block = w[q, at, :]
-            acc[q] += dot(x[:, at], block)
-            bacc[...] += dot(bg[q], block, NT)
-
-        aog[:, at] = bacc[...].astype(jnp.bfloat16)
-        store = pltpu.make_async_copy(aog.at[:, at], aog_hbm.at[:, at], local_sems.at[2 + len(stores)])
-        store.start()
-        stores.append(store)
-
-    big.own_end()
-    plane(place.z)
-    big.third(ORDER[0])
-    big.first(ORDER[2])
-    big.second(ORDER[1])
+    big.first(2, "l")
+    big.second(3, "l")
+    big.first(2, "u")
+    big.second(3, "u")
+    big.own_end(True)
+    unit(0, "d")
+    big.own_end(False)
+    unit(0, "e")
+    big.third(3)
+    unit(1, "a")
+    big.second(2, "l")
+    unit(1, "b")
 
     total = g_sum[pl.ds(2 * place.z, 2)]
     for i, k in enumerate(ORDER):
@@ -389,23 +446,29 @@
     y_send[...] = g_sum[2 * place.z + 1 - place.y].astype(jnp.bfloat16)
     post.send("ry", "y", y_send, y_got)
 
-    big.end(ORDER[0])
-    plane(place.far(ORDER[0]))
-    big.third(ORDER[1])
-    big.second(ORDER[2])
-
+    big.second(2, "u")
+    big.end(1, True)
+    unit(1, "d")
+    big.end(1, False)
+    unit(1, "e")
+    unit(3, "a")
     post.wait("ry", "y", y_got)
     half[...] = g_sum[place.f] + y_got[...].astype(jnp.float32)
     post.send("rx", "x", half, half_got)
-
-    big.end(ORDER[1])
-    plane(place.far(ORDER[1]))
+    unit(3, "b")
+    big.third(2)
+    unit(2, "a", True)
+    big.end(3, True)
+    unit(3, "d")
+    big.end(3, False)
+    unit(3, "e")
 
     post.wait("rx", "x", half_got)
     whole[place.c] = half[...] + half_got[...]
     post.send("rd", "c", whole.at[place.c])
-
-    big.third(ORDER[2])
+    big.end(2, True)
+    unit(2, "d", True)
+    unit(2, "b", True)
     post.wait("rd", "c", whole.at[1 - place.c])
     for i in range(rank // 32):
         r = i * 32
@@ -414,15 +477,8 @@
         dn_out[j * part : (j + 1) * part, :] = (
             whole[1, rank - hrows :, j * 128 : (j + 1) * 128] * scales[0]
         )
-
-    big.end(ORDER[2])
-    plane(place.far(ORDER[2]))
-    for q in range(4):
-        at = pl.ds(q * quarter, quarter)
-        mixed[:, at] = (acc[q] * grow[:, at]).astype(jnp.bfloat16)
-        store = pltpu.make_async_copy(mixed.at[:, at], mixed_hbm.at[:, at], local_sems.at[2 + len(stores)])
-        store.start()
-        stores.append(store)
+    big.end(2, False)
+    unit(2, "e", True)
     post.finish()
     for store in stores:
         store.wait()
@@ -435,7 +491,8 @@
     dp_count, fsdp_count = lax.axis_size("dp"), lax.axis_size("fsdp")
     per = gate.shape[0]
     sample = (lax.axis_index("dp") * fsdp_count) * tokens // PATCHES
-    step = lax.dynamic_slice_in_dim(timesteps, sample, 1).astype(jnp.float32)
+    chosen = jnp.arange(timesteps.shape[0], dtype=jnp.int32) == sample
+    step = jnp.sum(jnp.where(chosen, timesteps, 0)).astype(jnp.float32)
     number = lax.axis_index("fsdp") * per + jnp.arange(per, dtype=jnp.int32)
     half_freq = FREQ // 2
     frequency = jnp.exp(
@@ -468,7 +525,8 @@
             pltpu.VMEM((4, tokens, quarter), f32),
             pltpu.VMEM((tokens, width), bf),
             pltpu.VMEM((tokens, inner), bf),
-            pltpu.VMEM((tokens, 2 * rows), f32),
+            pltpu.VMEM((4, tokens, 2 * rows), f32),
+            pltpu.VMEM((tokens, rank), f32),
             pltpu.VMEM((rank, width), bf),
             pltpu.VMEM((inner, rank), bf),
             pltpu.VMEM((tokens, rank), bf),

time: 93.8 us -> 75.8 us (0.81)
  Pallas kernels: 84.2 us -> 66.7 us
  local copies, waits for them, and re-layouts: 6.85 us -> 5.54 us
  other arithmetic: 0.06 us -> 1.35 us
    pallas_call x1, Pallas kernels: 84.2 us -> 66.7 us  [fused(): pl.pallas_call(functools.partial(kernel, (gradient_scale, adapter_scale_f...]
    reduce_sum x0 -> x1, other arithmetic: none -> 1.29 us  [fused(): step = jnp.sum(jnp.where(chosen, timesteps, 0)).astype(jnp.float32)]
    dynamic_slice x1 -> x0, local copies, waits for them, and re-layouts: 1.24 us -> none  [fused(): step = lax.dynamic_slice_in_dim(timesteps, sample, 1).astype(jnp.float32)]
where the time goes in v2:
time: 75.8 us; the launch traced here: 75.6 us
  Pallas kernels  66.7 us (88%)
  local copies, waits for them, and re-layouts  5.54 us (7%)
  between operations  1.99 us (3%)
  other arithmetic  1.35 us (2%)
    pallas_call x1, Pallas kernels, fused(): pl.pallas_call(functools.partial(kernel, (gradient_scale, adapter_scale_f...  66.7 us
    unnamed x10, local copies, waits for them, and re-layouts  4.94 us

profile of v2, /device:TPU:0, one launch (start us, length us, event | category | flops | bytes accessed | tf_op | source)
XLA Modules:
  0.0 75.6 jit_solution(7727352977102077952)
XLA Ops:
  1.3 1.3 %fusion.1 = s32[]{:T(128)} fusion(s32[2]{0:T(128)} %param.15, s32[]{:T(128)S(6)} %select_n.27), kind=kLoop, calls=%fused_computation.6 | loop fusion | flops 5 | bytes 16 | tf_op jit(solution)/shard_map/reduce_sum | solution.py:495
  3.2 0.1 fusion
  3.3 0.6 broadcast_in_dim.15.feat
  3.9 66.7 %shard_map.111 = (bf16[256,3072]{1,0:T(8,128)(2,1)}, bf16[256,1536]{1,0:T(8,128)(2,1)}, f32[192,128]{1,0:T(8,128)}, f32[128,384]{1,0:T(8,128)}) custom-call(bf16[256,1536]{1,0:T(8,128)(2,1)} %x_hbm.1, bf16[256,3072]{1,0:T(8,128)(2,1)} %cot_hbm.1, bf16[192,3072]{1,0:T(8,128)(2,1)} %codes.1, bf16[1,1]{1,0:T(2,128)(2,1)} %bitcast.1.amax, ...), custom_call_target="tpu_custom_call" | custom-call | tf_op jit(solution)/shard_map/pallas_call | solution.py:509
  70.6 0.0 copy-start
  70.6 0.0 copy-start.2
  70.6 2.7 %copy.17 = bf16[256,3072]{1,0:T(8,128)(2,1)} copy(bf16[256,3072]{1,0:T(8,128)(2,1)} %get-tuple-element.8) | data formatting | bytes 3145728
  73.3 0.0 copy-done
  73.3 0.0 copy-start.1
  73.4 0.9 %copy.18 = bf16[256,1536]{1,0:T(8,128)(2,1)} copy(bf16[256,1536]{1,0:T(8,128)(2,1)S(1)} %copy-done) | data formatting | bytes 1572864
  74.2 0.0 copy-done.2
  74.2 0.6 copy.19
  74.9 0.0 copy-done.1
  74.9 0.7 copy.20
Async XLA Ops:
  70.6 2.8 %copy-start = (bf16[256,1536]{1,0:T(8,128)(2,1)S(1)}, bf16[256,1536]{1,0:T(8,128)(2,1)}, u32[]{:S(2)}) copy-start(bf16[256,1536]{1,0:T(8,128)(2,1)} %get-tuple-element.9) | copy-start | bytes 2359300
  70.6 3.6 %copy-start.2 = (f32[192,128]{1,0:T(8,128)S(1)}, f32[192,128]{1,0:T(8,128)}, u32[]{:S(2)}) copy-start(f32[192,128]{1,0:T(8,128)} %get-tuple-element.10) | copy-start | bytes 294916
  73.3 1.5 %copy-start.1 = (f32[128,384]{1,0:T(8,128)S(1)}, f32[128,384]{1,0:T(8,128)}, u32[]{:S(2)}) copy-start(f32[128,384]{1,0:T(8,128)} %get-tuple-element.11) | copy-start | bytes 589828

commit v3 on v2

--- a/solution.py
+++ b/solution.py
@@ -104,6 +104,7 @@
         self.dp, self.f = lax.axis_index("dp"), lax.axis_index("fsdp")
         self.c, self.x = lax.rem(self.dp, 2), lax.rem(lax.div(self.dp, 2), 2)
         self.y, self.z = lax.rem(self.f, 2), lax.div(self.f, 2)
+        self.inner = lax.rem(self.z + 1, 4) > 1
 
     def far(self, k):
         z = self.z
@@ -112,6 +113,12 @@
         if k == 2:
             return z + 2 - 4 * lax.div(z, 2)
         return 3 - z
+
+    def plane(self, k):
+        upper = lax.div(self.z, 2)
+        if k == 1:
+            return self.far(1)
+        return 2 - upper if k == 2 else 3 - 3 * upper
 
     def device(self, way):
         if way == "c":
@@ -126,14 +133,15 @@
 class Post:
     def __init__(self, place, send_sems, recv_sems):
         self.place, self.ss, self.rs = place, send_sems, recv_sems
-        self.index, self.sent = {}, []
-
-    def _copy(self, name, way, src, dst):
+        self.index, self.sent, self.sent_inner = {}, [], []
+
+    def _copy(self, name, way, src, dst, sender=None):
         i = self.index.setdefault(name, len(self.index))
+        j = self.index.setdefault(sender or name, len(self.index))
         return pltpu.make_async_remote_copy(
             src_ref=src,
             dst_ref=dst,
-            send_sem=self.ss.at[i],
+            send_sem=self.ss.at[j],
             recv_sem=self.rs.at[i],
             device_id=self.place.device(way),
             device_id_type=MESH,
@@ -144,6 +152,11 @@
         copy.start()
         self.sent.append(copy)
 
+    def send_inner(self, name, way, src, sender):
+        copy = self._copy(name, way, src, src, sender)
+        pl.when(self.place.inner)(copy.start)
+        self.sent_inner.append(copy)
+
     def wait(self, name, way, dst):
         self._copy(name, way, dst, dst).wait_recv()
 
@@ -151,10 +164,16 @@
         for copy in self.sent:
             copy.wait_send()
 
+        @pl.when(self.place.inner)
+        def _():
+            for copy in self.sent_inner:
+                copy.wait_send()
+
 
 class Gather:
-    def __init__(self, tag, post, place, piece):
+    def __init__(self, tag, post, place, piece, chain):
         self.tag, self.post, self.p, self.piece = tag, post, place, piece
+        self.chain, self.far = chain, place.plane if chain else place.far
 
     def send(self, name, way, region):
         self.post.send((self.tag, name), way, region)
@@ -170,7 +189,14 @@
     def start(self, k):
         p = self.p
         for h in "lu":
-            self.send(("z", k, h), k, self.piece(p.c, p.x, p.z, p.y, h))
+            own = self.piece(p.c, p.x, p.z, p.y, h)
+            if self.chain and k == 3:
+                self.relay(2, k, own, h, "own")
+            else:
+                self.send(("z", k, h), k, own)
+
+    def relay(self, k, way, region, h, why):
+        self.post.send_inner((self.tag, ("z", k, h)), way, region, (self.tag, why, k, h))
 
     def own_first(self, h):
         p = self.p
@@ -195,15 +221,20 @@
 
     def first(self, k, h):
         p = self.p
-        got = self.piece(p.c, p.x, p.far(k), p.y, h)
+        got = self.piece(p.c, p.x, self.far(k), p.y, h)
         self.wait(("z", k, h), k, got)
+        if self.chain:
+            if k == 1:
+                self.relay(3, 3, got, h, "across")
+            else:
+                self.relay(k, 1, got, h, "out")
         self.send(("x", k, h), "x", got)
         self.send(("y", k, h), "y", got)
         self.send(("c1", k, h), "c", got)
 
     def second(self, k, h):
         p = self.p
-        zz = p.far(k)
+        zz = self.far(k)
         got = self.piece(p.c, p.x, zz, 1 - p.y, h)
         self.wait(("y", k, h), "y", got)
         if h == "u":
@@ -218,13 +249,13 @@
     def third(self, k):
         p = self.p
         for h in "lu":
-            got = self.piece(p.c, 1 - p.x, p.far(k), 1 - p.y, h)
+            got = self.piece(p.c, 1 - p.x, self.far(k), 1 - p.y, h)
             self.wait(("d", k, h), "y" if h == "l" else "x", got)
             self.send(("c4", k, h), "c", got)
 
     def end(self, k, same):
         p = self.p
-        zz, c = p.far(k), 1 - p.c
+        zz, c = self.far(k), 1 - p.c
         for h in "lu":
             if same:
                 self.wait(("c1", k, h), "c", self.piece(c, p.x, zz, p.y, h))
@@ -234,15 +265,15 @@
                 self.wait(("c4", k, h), "c", self.piece(c, 1 - p.x, zz, 1 - p.y, h))
 
 
-MESSAGES = 2 * (16 * len(ORDER) + 8) + 4 + 7
+MESSAGES = 2 * (16 * len(ORDER) + 8) + 4 + 7 + 8
 
 
 def kernel(
-    scales,
-    x_hbm, cot_hbm, codes, amax, down, up, gate, feat,
+    scales, samples,
+    x_hbm, cot_hbm, codes, down, up, gate, feat,
     mixed_hbm, aog_hbm, dn_out, up_out,
     w, pre, x, cot, bg, acc, mixed, aog, bacc, bsum, upf, downf, lr, bn, grow,
-    gates, gf, g_send, g_got, g_sum, z_send, z_got, y_send, y_got, half, half_got, whole,
+    partial, gates, gf, g_send, g_got, g_sum, z_send, z_got, y_send, y_got, half, half_got, whole,
     send_sems, recv_sems, local_sems,
 ):
     place = Place()
@@ -273,15 +304,18 @@
         begin = pl.multiple_of((2 * c + xx) * 48 + start, 16)
         return pre.at[2 * zz + yy, pl.ds(begin, size)]
 
-    big = Gather("w", post, place, w_piece)
-    small = Gather("p", post, place, pre_piece)
+    big = Gather("w", post, place, w_piece, True)
+    small = Gather("p", post, place, pre_piece, False)
     own = pl.ds(pl.multiple_of(place.f * rows, rows), rows)
-    factor = amax[...].astype(jnp.float32)
+    per = gate.shape[0]
+    factor = feat[0:1, per : per + 1]
 
     pre[place.f, :rank, :] = up[...]
     for j in range(3):
         pre[place.f, rank:, j * 128 : (j + 1) * 128] = down[j * part : (j + 1) * part, :]
-    gates[0] = dot(feat[...], gate[...])[0:1]
+    partial[...] = dot(feat[:, :per].astype(jnp.bfloat16), gate[...])
+    sample = lax.div(place.dp * samples[0], samples[1])
+    gates[0] = partial[pl.ds(sample, 1), :]
 
     def scale(q):
         columns = pl.ds(pl.multiple_of(q * quarter, 128), quarter)
@@ -316,9 +350,11 @@
     for k in ORDER:
         for h in "lu":
             small.second(k, h)
+    big.first(1, "l")
     big.own_first("u")
     for k in ORDER:
         small.third(k)
+    big.first(1, "u")
     for i, k in enumerate(ORDER):
         post.wait(("gz", k), k, gates.at[3 + i])
     grow[...] = gates[2] + gates[3] + gates[4] + gates[5]
@@ -336,11 +372,9 @@
 
     load_x.wait()
     load_cot.wait()
-    big.first(1, "l")
     lr[...] = dot(x[...], downf[...]).astype(jnp.bfloat16)
     bsum[...] = jnp.zeros_like(bsum)
-    big.first(1, "u")
-    big.start(2)
+    big.own_second("l")
 
     def adapter(begin, end):
         @pl.loop(begin, end)
@@ -356,10 +390,12 @@
             gf[2 * q + 1, :rank, :] = term[:, shard_up:]
 
     adapter(0, 2)
-    big.own_second("l")
+    big.first(2, "l")
+    big.first(2, "u")
     big.own_second("u")
+    big.second(1, "l")
     adapter(2, 4)
-    big.second(1, "l")
+    big.second(1, "u")
     bn[...] = (0.5 * bsum[...]).astype(jnp.bfloat16)
 
     @pl.loop(0, 4)
@@ -391,7 +427,7 @@
     }
 
     def unit(k, which, last=False):
-        zz = place.far(k) if k else place.z
+        zz = place.plane(k) if k else place.z
         q = quarters[which]
         at = pl.ds(pl.multiple_of(zz * 2 * rows, 128), 2 * rows)
         block = w[q, at, :]
@@ -414,7 +450,6 @@
 
     big.first(3, "l")
     big.first(3, "u")
-    big.second(1, "u")
     unit(0, "a")
     unit(0, "b")
     big.third(1)
@@ -425,17 +460,15 @@
     for i, k in enumerate(ORDER):
         post.send(("rz", k), k, z_send.at[pl.ds(2 * place.far(k), 2)], z_got.at[i])
 
-    big.first(2, "l")
-    big.second(3, "l")
-    big.first(2, "u")
-    big.second(3, "u")
+    big.second(2, "l")
     big.own_end(True)
     unit(0, "d")
+    big.second(2, "u")
     big.own_end(False)
     unit(0, "e")
-    big.third(3)
     unit(1, "a")
-    big.second(2, "l")
+    big.third(2)
+    big.second(3, "l")
     unit(1, "b")
 
     total = g_sum[pl.ds(2 * place.z, 2)]
@@ -446,29 +479,29 @@
     y_send[...] = g_sum[2 * place.z + 1 - place.y].astype(jnp.bfloat16)
     post.send("ry", "y", y_send, y_got)
 
-    big.second(2, "u")
+    big.second(3, "u")
     big.end(1, True)
     unit(1, "d")
     big.end(1, False)
     unit(1, "e")
-    unit(3, "a")
+    unit(2, "a")
     post.wait("ry", "y", y_got)
     half[...] = g_sum[place.f] + y_got[...].astype(jnp.float32)
     post.send("rx", "x", half, half_got)
-    unit(3, "b")
-    big.third(2)
-    unit(2, "a", True)
-    big.end(3, True)
-    unit(3, "d")
-    big.end(3, False)
-    unit(3, "e")
+    big.third(3)
+    unit(2, "b")
+    big.end(2, True)
+    unit(2, "d")
+    big.end(2, False)
+    unit(2, "e")
 
     post.wait("rx", "x", half_got)
     whole[place.c] = half[...] + half_got[...]
     post.send("rd", "c", whole.at[place.c])
-    big.end(2, True)
-    unit(2, "d", True)
-    unit(2, "b", True)
+    unit(3, "a", True)
+    unit(3, "b", True)
+    big.end(3, True)
+    unit(3, "d", True)
     post.wait("rd", "c", whole.at[1 - place.c])
     for i in range(rank // 32):
         r = i * 32
@@ -477,11 +510,29 @@
         dn_out[j * part : (j + 1) * part, :] = (
             whole[1, rank - hrows :, j * 128 : (j + 1) * 128] * scales[0]
         )
-    big.end(2, False)
-    unit(2, "e", True)
+    big.end(3, False)
+    unit(3, "e", True)
     post.finish()
     for store in stores:
         store.wait()
+
+
+def hand_over(mixed, aog, dn, up, mixed_out, aog_out, dn_out, up_out, sems):
+    copies = []
+    for source, target, parts in (
+        (mixed, mixed_out, 4),
+        (aog, aog_out, 2),
+        (dn, dn_out, 1),
+        (up, up_out, 1),
+    ):
+        size = source.shape[0] // parts
+        for i in range(parts):
+            at = pl.ds(i * size, size)
+            copies.append(pltpu.make_async_copy(source.at[at], target.at[at], sems.at[len(copies)]))
+    for copy in copies:
+        copy.start()
+    for copy in copies:
+        copy.wait()
 
 
 def fused(x, cot, codes, amax, down, up, gate, timesteps):
@@ -490,31 +541,34 @@
     rows = codes.shape[0]
     dp_count, fsdp_count = lax.axis_size("dp"), lax.axis_size("fsdp")
     per = gate.shape[0]
-    sample = (lax.axis_index("dp") * fsdp_count) * tokens // PATCHES
-    chosen = jnp.arange(timesteps.shape[0], dtype=jnp.int32) == sample
-    step = jnp.sum(jnp.where(chosen, timesteps, 0)).astype(jnp.float32)
-    number = lax.axis_index("fsdp") * per + jnp.arange(per, dtype=jnp.int32)
+    shape = (timesteps.shape[0], 2 * per)
+    column = lax.broadcasted_iota(jnp.int32, shape, 1)
+    number = lax.axis_index("fsdp") * per + column
     half_freq = FREQ // 2
     frequency = jnp.exp(
         -math.log(10000.0) * (number % half_freq).astype(jnp.float32) / half_freq
     )
-    angle = step * frequency
-    feat = jnp.where(number < half_freq, jnp.cos(angle), jnp.sin(angle)).astype(jnp.bfloat16)
-    feat = jnp.broadcast_to(feat[None, :], (16, per))
+    angle = timesteps.astype(jnp.float32)[:, None] * frequency
+    feat = jnp.where(number < half_freq, jnp.cos(angle), jnp.sin(angle))
+    feat = jnp.where(column < per, feat, amax.astype(jnp.float32)[:, None])
     gradient_scale = (tokens * dp_count * fsdp_count) ** (-0.5)
     bf, f32 = jnp.bfloat16, jnp.float32
     quarter, hrows = width // 4, rows // 2
     vmem = pl.BlockSpec(memory_space=pltpu.VMEM)
     hbm = pl.BlockSpec(memory_space=pl.ANY)
-    return pl.pallas_call(
-        functools.partial(kernel, (gradient_scale, adapter_scale_factor * gradient_scale)),
+    results = pl.pallas_call(
+        functools.partial(
+            kernel,
+            (gradient_scale, adapter_scale_factor * gradient_scale),
+            (fsdp_count * tokens, PATCHES),
+        ),
         out_shape=(
             jax.ShapeDtypeStruct((tokens, width), bf),
             jax.ShapeDtypeStruct((tokens, inner), bf),
             jax.ShapeDtypeStruct((rows, rank), f32),
             jax.ShapeDtypeStruct((rank, up.shape[1]), f32),
         ),
-        in_specs=[hbm, hbm] + [vmem] * 6,
+        in_specs=[hbm, hbm] + [vmem] * 5,
         out_specs=(hbm, hbm, vmem, vmem),
         scratch_shapes=[
             pltpu.VMEM((4, inner, quarter), bf),
@@ -532,6 +586,7 @@
             pltpu.VMEM((tokens, rank), bf),
             pltpu.VMEM((tokens, rank), bf),
             pltpu.VMEM((1, width), f32),
+            pltpu.VMEM((timesteps.shape[0], width), f32),
             pltpu.VMEM((6, 1, width), f32),
             pltpu.VMEM((8, rows, up.shape[1]), f32),
             pltpu.VMEM((8, hrows, up.shape[1]), bf),
@@ -551,7 +606,15 @@
         compiler_params=pltpu.CompilerParams(
             collective_id=0, has_side_effects=True, vmem_limit_bytes=56 * 1024 * 1024
         ),
-    )(x, cot, codes, amax[None, :], down, up, gate, feat)
+    )(x, cot, codes, down, up, gate, feat)
+    return pl.pallas_call(
+        hand_over,
+        out_shape=tuple(jax.ShapeDtypeStruct(r.shape, r.dtype) for r in results),
+        in_specs=[hbm] * 4,
+        out_specs=(hbm,) * 4,
+        scratch_shapes=[pltpu.SemaphoreType.DMA((10,))],
+        compiler_params=pltpu.CompilerParams(vmem_limit_bytes=60 * 1024 * 1024),
+    )(*results)
 
 
 def fits(mesh):

time: 75.8 us -> 152 us (2.01)
  Pallas kernels: 66.7 us -> 149 us
  local copies, waits for them, and re-layouts: 5.54 us -> 0 us
    pallas_call x0 -> x1, Pallas kernels: none -> 81.6 us  [fused(): pl.pallas_call(hand_over, out_shape=tuple((jax.ShapeDtypeStruct(r.shape,...]
    unnamed x10 -> x0, local copies, waits for them, and re-layouts: 4.94 us -> none
where the time goes in v3:
time: 152 us
  Pallas kernels  149 us (98%)
    pallas_call x1, Pallas kernels, fused(): pl.pallas_call(hand_over, out_shape=tuple((jax.ShapeDtypeStruct(r.shape,...  81.6 us
    pallas_call x1, Pallas kernels, fused(): pl.pallas_call(functools.partial(kernel, (gradient_scale, adapter_scale_f...  67.4 us

profile of v3, /device:TPU:0, one launch (start us, length us, event | category | flops | bytes accessed | tf_op | source)
XLA Modules:
  0.0 151.6 jit_solution(7217068803395278291)
XLA Ops:
  1.3 0.7 convert_element_type.7
  2.0 0.7 select_select_fusion.feat
  2.7 67.4 %shard_map.111 = (bf16[256,3072]{1,0:T(8,128)(2,1)}, bf16[256,1536]{1,0:T(8,128)(2,1)}, f32[192,128]{1,0:T(8,128)}, f32[128,384]{1,0:T(8,128)}) custom-call(bf16[256,1536]{1,0:T(8,128)(2,1)} %x_hbm.1, bf16[256,3072]{1,0:T(8,128)(2,1)} %cot_hbm.1, bf16[192,3072]{1,0:T(8,128)(2,1)} %codes.1, bf16[192,128]{1,0:T(8,128)(2,1)} %down.1, bf16[128,384]{1,0:T(8,128)(2,1)} %up.1, ...), custom_call_target="tpu_custom_call" | custom-call | tf_op jit(solution)/shard_map/pallas_call | solution.py:559
  70.0 81.6 %shard_map.112 = (bf16[256,3072]{1,0:T(8,128)(2,1)}, bf16[256,1536]{1,0:T(8,128)(2,1)}, f32[192,128]{1,0:T(8,128)}, f32[128,384]{1,0:T(8,128)}) custom-call(bf16[256,3072]{1,0:T(8,128)(2,1)} %get-tuple-element.8.mixed, bf16[256,1536]{1,0:T(8,128)(2,1)} %get-tuple-element.9.aog, f32[192,128]{1,0:T(8,128)} %get-tuple-element.10.dn, ...), custom_call_target="tpu_custom_call" | custom-call | tf_op jit(solution)/shard_map/pallas_call | solution.py:610
  (3 shorter events, 0.0 us)

commit v4 on v3

--- a/solution.py
+++ b/solution.py
@@ -186,10 +186,16 @@
         for h in "lu":
             self.send(("oy", h), "y", self.piece(p.c, p.x, p.z, p.y, h))
 
-    def start(self, k):
-        p = self.p
-        for h in "lu":
-            own = self.piece(p.c, p.x, p.z, p.y, h)
+    def part(self, zz, yy, h):
+        p = self.p
+        if h == "e":
+            return self.piece(p.c, 1 - p.x, zz, yy, "u")
+        return self.piece(p.c, p.x, zz, yy, h)
+
+    def start(self, k, parts="lue"):
+        p = self.p
+        for h in parts:
+            own = self.part(p.z, p.y, h)
             if self.chain and k == 3:
                 self.relay(2, k, own, h, "own")
             else:
@@ -220,15 +226,20 @@
                 self.wait(("oc2", h), "c", self.piece(1 - p.c, 1 - p.x, p.z, 1 - p.y, h))
 
     def first(self, k, h):
-        p = self.p
-        got = self.piece(p.c, p.x, self.far(k), p.y, h)
+        got = self.part(self.far(k), self.p.y, h)
         self.wait(("z", k, h), k, got)
         if self.chain:
             if k == 1:
                 self.relay(3, 3, got, h, "across")
             else:
                 self.relay(k, 1, got, h, "out")
-        self.send(("x", k, h), "x", got)
+        if h == "e":
+            if k != 1:
+                self.send(("d", k, "u"), "y", got)
+            self.send(("c2", k, "u"), "c", got)
+            return
+        if h == "l":
+            self.send(("x", k), "x", got)
         self.send(("y", k, h), "y", got)
         self.send(("c1", k, h), "c", got)
 
@@ -237,20 +248,19 @@
         zz = self.far(k)
         got = self.piece(p.c, p.x, zz, 1 - p.y, h)
         self.wait(("y", k, h), "y", got)
-        if h == "u":
+        if h == "l" or k == 1:
             self.send(("d", k, h), "x", got)
         self.send(("c3", k, h), "c", got)
-        got = self.piece(p.c, 1 - p.x, zz, p.y, h)
-        self.wait(("x", k, h), "x", got)
         if h == "l":
-            self.send(("d", k, h), "y", got)
-        self.send(("c2", k, h), "c", got)
+            got = self.piece(p.c, 1 - p.x, zz, p.y, h)
+            self.wait(("x", k), "x", got)
+            self.send(("c2", k, h), "c", got)
 
     def third(self, k):
         p = self.p
         for h in "lu":
             got = self.piece(p.c, 1 - p.x, self.far(k), 1 - p.y, h)
-            self.wait(("d", k, h), "y" if h == "l" else "x", got)
+            self.wait(("d", k, h), "x" if h == "l" or k == 1 else "y", got)
             self.send(("c4", k, h), "c", got)
 
     def end(self, k, same):
@@ -265,7 +275,7 @@
                 self.wait(("c4", k, h), "c", self.piece(c, 1 - p.x, zz, 1 - p.y, h))
 
 
-MESSAGES = 2 * (16 * len(ORDER) + 8) + 4 + 7 + 8
+MESSAGES = 2 * (16 * len(ORDER) + 8) + 4 + 7 + 12
 
 
 def kernel(
@@ -329,11 +339,14 @@
     small.start_own()
     for k in ORDER:
         small.start(k)
-    big.start(1)
+    big.start(1, "lu")
     big.start_own()
-    big.start(3)
-    for i in range(1, 4):
-        scale(lax.rem(mine + i, 4))
+    big.start(3, "lu")
+    scale(2 * place.c + 1 - place.x)
+    big.start(1, "e")
+    big.start(3, "e")
+    scale(2 - 2 * place.c)
+    scale(3 - 2 * place.c)
 
     post.wait("gy", "y", gates.at[1])
     gates[2] = gates[0] + gates[1]
@@ -342,7 +355,7 @@
     for h in "lu":
         small.own_first(h)
     for k in ORDER:
-        for h in "lu":
+        for h in "lue":
             small.first(k, h)
     big.own_first("l")
     for h in "lu":
@@ -355,6 +368,7 @@
     for k in ORDER:
         small.third(k)
     big.first(1, "u")
+    big.first(1, "e")
     for i, k in enumerate(ORDER):
         post.wait(("gz", k), k, gates.at[3 + i])
     grow[...] = gates[2] + gates[3] + gates[4] + gates[5]
@@ -392,6 +406,7 @@
     adapter(0, 2)
     big.first(2, "l")
     big.first(2, "u")
+    big.first(2, "e")
     big.own_second("u")
     big.second(1, "l")
     adapter(2, 4)
@@ -450,6 +465,7 @@
 
     big.first(3, "l")
     big.first(3, "u")
+    big.first(3, "e")
     unit(0, "a")
     unit(0, "b")
     big.third(1)
@@ -517,22 +533,30 @@
         store.wait()
 
 
-def hand_over(mixed, aog, dn, up, mixed_out, aog_out, dn_out, up_out, sems):
-    copies = []
-    for source, target, parts in (
-        (mixed, mixed_out, 4),
-        (aog, aog_out, 2),
-        (dn, dn_out, 1),
-        (up, up_out, 1),
+def hand_over(mixed, aog, dn, up, mixed_out, aog_out, dn_out, up_out, mixed_v, aog_v, dn_v, up_v, sems):
+    steps = []
+    for source, held, target, parts in (
+        (mixed, mixed_v, mixed_out, 4),
+        (aog, aog_v, aog_out, 2),
+        (dn, dn_v, dn_out, 1),
+        (up, up_v, up_out, 1),
     ):
         size = source.shape[0] // parts
         for i in range(parts):
-            at = pl.ds(i * size, size)
-            copies.append(pltpu.make_async_copy(source.at[at], target.at[at], sems.at[len(copies)]))
-    for copy in copies:
-        copy.start()
-    for copy in copies:
-        copy.wait()
+            at, n = pl.ds(i * size, size), 2 * len(steps)
+            steps.append(
+                (
+                    pltpu.make_async_copy(source.at[at], held.at[at], sems.at[n]),
+                    pltpu.make_async_copy(held.at[at], target.at[at], sems.at[n + 1]),
+                )
+            )
+    for fetch, _ in steps:
+        fetch.start()
+    for fetch, store in steps:
+        fetch.wait()
+        store.start()
+    for _, store in steps:
+        store.wait()
 
 
 def fused(x, cot, codes, amax, down, up, gate, timesteps):
@@ -612,7 +636,8 @@
         out_shape=tuple(jax.ShapeDtypeStruct(r.shape, r.dtype) for r in results),
         in_specs=[hbm] * 4,
         out_specs=(hbm,) * 4,
-        scratch_shapes=[pltpu.SemaphoreType.DMA((10,))],
+        scratch_shapes=[pltpu.VMEM(r.shape, r.dtype) for r in results]
+        + [pltpu.SemaphoreType.DMA((16,))],
         compiler_params=pltpu.CompilerParams(vmem_limit_bytes=60 * 1024 * 1024),
     )(*results)
 

time: 152 us -> 77.2 us (0.51)
  Pallas kernels: 149 us -> 73.1 us
    pallas_call x1, Pallas kernels: 81.6 us -> 2.62 us  [fused(): pl.pallas_call(hand_over, out_shape=tuple((jax.ShapeDtypeStruct(r.shape,...]
    pallas_call x1, Pallas kernels: 67.4 us -> 70.5 us  [fused(): pl.pallas_call(functools.partial(kernel, (gradient_scale, adapter_scale_f...]
where the time goes in v4:
time: 77.2 us; the launch traced here: 75.8 us
  Pallas kernels  73.1 us (95%)
  other arithmetic  1.37 us (2%)
  between operations  1.31 us (2%)
    pallas_call x1, Pallas kernels, fused(): pl.pallas_call(functools.partial(kernel, (gradient_scale, adapter_scale_f...  70.5 us
    pallas_call x1, Pallas kernels, fused(): pl.pallas_call(hand_over, out_shape=tuple((jax.ShapeDtypeStruct(r.shape,...  2.62 us

profile of v4, /device:TPU:0, one launch (start us, length us, event | category | flops | bytes accessed | tf_op | source)
XLA Modules:
  0.0 75.8 jit_solution(7200715125192755011)
XLA Ops:
  1.3 0.7 convert_element_type.7
  2.0 0.7 select_select_fusion.feat
  2.7 70.5 %shard_map.111 = (bf16[256,3072]{1,0:T(8,128)(2,1)}, bf16[256,1536]{1,0:T(8,128)(2,1)}, f32[192,128]{1,0:T(8,128)}, f32[128,384]{1,0:T(8,128)}) custom-call(bf16[256,1536]{1,0:T(8,128)(2,1)} %x_hbm.1, bf16[256,3072]{1,0:T(8,128)(2,1)} %cot_hbm.1, bf16[192,3072]{1,0:T(8,128)(2,1)} %codes.1, bf16[192,128]{1,0:T(8,128)(2,1)} %down.1, bf16[128,384]{1,0:T(8,128)(2,1)} %up.1, ...), custom_call_target="tpu_custom_call" | custom-call | tf_op jit(solution)/shard_map/pallas_call | solution.py:583
  73.2 2.6 %shard_map.112 = (bf16[256,3072]{1,0:T(8,128)(2,1)}, bf16[256,1536]{1,0:T(8,128)(2,1)}, f32[192,128]{1,0:T(8,128)}, f32[128,384]{1,0:T(8,128)}) custom-call(bf16[256,3072]{1,0:T(8,128)(2,1)} %get-tuple-element.8.mixed, bf16[256,1536]{1,0:T(8,128)(2,1)} %get-tuple-element.9.aog, f32[192,128]{1,0:T(8,128)} %get-tuple-element.10.dn, ...), custom_call_target="tpu_custom_call" | custom-call | tf_op jit(solution)/shard_map/pallas_call | solution.py:634
  (3 shorter events, 0.0 us)

commit v5 on v3

--- a/solution.py
+++ b/solution.py
@@ -329,32 +329,28 @@
     small.start_own()
     for k in ORDER:
         small.start(k)
-    big.start(1)
-    big.start_own()
-    big.start(3)
     for i in range(1, 4):
         scale(lax.rem(mine + i, 4))
 
+    for h in "lu":
+        small.own_first(h)
     post.wait("gy", "y", gates.at[1])
     gates[2] = gates[0] + gates[1]
     for i, k in enumerate(ORDER):
         post.send(("gz", k), k, gates.at[2], gates.at[3 + i])
-    for h in "lu":
-        small.own_first(h)
     for k in ORDER:
         for h in "lu":
             small.first(k, h)
-    big.own_first("l")
+    big.start(1)
+    big.start_own()
+    big.start(3)
     for h in "lu":
         small.own_second(h)
     for k in ORDER:
         for h in "lu":
             small.second(k, h)
-    big.first(1, "l")
-    big.own_first("u")
     for k in ORDER:
         small.third(k)
-    big.first(1, "u")
     for i, k in enumerate(ORDER):
         post.wait(("gz", k), k, gates.at[3 + i])
     grow[...] = gates[2] + gates[3] + gates[4] + gates[5]
@@ -370,11 +366,14 @@
             to = pl.ds(pl.multiple_of(f * rows + j * part, part), part)
             downf[to, :] = pre[f, rank:, j * 128 : (j + 1) * 128]
 
+    big.own_first("l")
+    big.first(1, "l")
     load_x.wait()
     load_cot.wait()
     lr[...] = dot(x[...], downf[...]).astype(jnp.bfloat16)
     bsum[...] = jnp.zeros_like(bsum)
-    big.own_second("l")
+    big.own_first("u")
+    big.first(1, "u")
 
     def adapter(begin, end):
         @pl.loop(begin, end)
@@ -390,12 +389,12 @@
             gf[2 * q + 1, :rank, :] = term[:, shard_up:]
 
     adapter(0, 2)
+    big.own_second("l")
     big.first(2, "l")
+    adapter(2, 4)
     big.first(2, "u")
     big.own_second("u")
     big.second(1, "l")
-    adapter(2, 4)
-    big.second(1, "u")
     bn[...] = (0.5 * bsum[...]).astype(jnp.bfloat16)
 
     @pl.loop(0, 4)
@@ -448,9 +447,10 @@
         else:
             acc[q] = total
 
+    big.second(1, "u")
+    unit(0, "a")
     big.first(3, "l")
     big.first(3, "u")
-    unit(0, "a")
     unit(0, "b")
     big.third(1)
 
@@ -517,22 +517,30 @@
         store.wait()
 
 
-def hand_over(mixed, aog, dn, up, mixed_out, aog_out, dn_out, up_out, sems):
-    copies = []
-    for source, target, parts in (
-        (mixed, mixed_out, 4),
-        (aog, aog_out, 2),
-        (dn, dn_out, 1),
-        (up, up_out, 1),
+def hand_over(mixed, aog, dn, up, mixed_out, aog_out, dn_out, up_out, mixed_v, aog_v, dn_v, up_v, sems):
+    steps = []
+    for source, held, target, parts in (
+        (mixed, mixed_v, mixed_out, 4),
+        (aog, aog_v, aog_out, 2),
+        (dn, dn_v, dn_out, 1),
+        (up, up_v, up_out, 1),
     ):
         size = source.shape[0] // parts
         for i in range(parts):
-            at = pl.ds(i * size, size)
-            copies.append(pltpu.make_async_copy(source.at[at], target.at[at], sems.at[len(copies)]))
-    for copy in copies:
-        copy.start()
-    for copy in copies:
-        copy.wait()
+            at, n = pl.ds(i * size, size), 2 * len(steps)
+            steps.append(
+                (
+                    pltpu.make_async_copy(source.at[at], held.at[at], sems.at[n]),
+                    pltpu.make_async_copy(held.at[at], target.at[at], sems.at[n + 1]),
+                )
+            )
+    for fetch, _ in steps:
+        fetch.start()
+    for fetch, store in steps:
+        fetch.wait()
+        store.start()
+    for _, store in steps:
+        store.wait()
 
 
 def fused(x, cot, codes, amax, down, up, gate, timesteps):
@@ -612,7 +620,8 @@
         out_shape=tuple(jax.ShapeDtypeStruct(r.shape, r.dtype) for r in results),
         in_specs=[hbm] * 4,
         out_specs=(hbm,) * 4,
-        scratch_shapes=[pltpu.SemaphoreType.DMA((10,))],
+        scratch_shapes=[pltpu.VMEM(r.shape, r.dtype) for r in results]
+        + [pltpu.SemaphoreType.DMA((16,))],
         compiler_params=pltpu.CompilerParams(vmem_limit_bytes=60 * 1024 * 1024),
     )(*results)
 

time: 152 us -> 81.5 us (0.54)
  Pallas kernels: 149 us -> 78.7 us
    pallas_call x1, Pallas kernels: 81.6 us -> 2.62 us  [fused(): pl.pallas_call(hand_over, out_shape=tuple((jax.ShapeDtypeStruct(r.shape,...]
    pallas_call x1, Pallas kernels: 67.4 us -> 76 us  [fused(): pl.pallas_call(functools.partial(kernel, (gradient_scale, adapter_scale_f...]
where the time goes in v5:
time: 81.5 us; the launch traced here: 81.3 us
  Pallas kernels  78.7 us (97%)
  other arithmetic  1.37 us (2%)
  between operations  1.31 us (2%)
    pallas_call x1, Pallas kernels, fused(): pl.pallas_call(functools.partial(kernel, (gradient_scale, adapter_scale_f...  76 us
    pallas_call x1, Pallas kernels, fused(): pl.pallas_call(hand_over, out_shape=tuple((jax.ShapeDtypeStruct(r.shape,...  2.62 us

profile of v5, /device:TPU:0, one launch (start us, length us, event | category | flops | bytes accessed | tf_op | source)
XLA Modules:
  0.0 81.3 jit_solution(7763926081816535418)
XLA Ops:
  1.3 0.7 convert_element_type.7
  2.0 0.7 select_select_fusion.feat
  2.7 76.0 %shard_map.111 = (bf16[256,3072]{1,0:T(8,128)(2,1)}, bf16[256,1536]{1,0:T(8,128)(2,1)}, f32[192,128]{1,0:T(8,128)}, f32[128,384]{1,0:T(8,128)}) custom-call(bf16[256,1536]{1,0:T(8,128)(2,1)} %x_hbm.1, bf16[256,3072]{1,0:T(8,128)(2,1)} %cot_hbm.1, bf16[192,3072]{1,0:T(8,128)(2,1)} %codes.1, bf16[192,128]{1,0:T(8,128)(2,1)} %down.1, bf16[128,384]{1,0:T(8,128)(2,1)} %up.1, ...), custom_call_target="tpu_custom_call" | custom-call | tf_op jit(solution)/shard_map/pallas_call | solution.py:567
  78.7 2.6 %shard_map.112 = (bf16[256,3072]{1,0:T(8,128)(2,1)}, bf16[256,1536]{1,0:T(8,128)(2,1)}, f32[192,128]{1,0:T(8,128)}, f32[128,384]{1,0:T(8,128)}) custom-call(bf16[256,3072]{1,0:T(8,128)(2,1)} %get-tuple-element.8.mixed, bf16[256,1536]{1,0:T(8,128)(2,1)} %get-tuple-element.9.aog, f32[192,128]{1,0:T(8,128)} %get-tuple-element.10.dn, ...), custom_call_target="tpu_custom_call" | custom-call | tf_op jit(solution)/shard_map/pallas_call | solution.py:618
  (3 shorter events, 0.0 us)

commit v6 on v2

--- a/solution.py
+++ b/solution.py
@@ -238,11 +238,11 @@
 
 
 def kernel(
-    scales,
-    x_hbm, cot_hbm, codes, amax, down, up, gate, feat,
+    scales, samples,
+    x_hbm, cot_hbm, codes, down, up, gate, feat,
     mixed_hbm, aog_hbm, dn_out, up_out,
     w, pre, x, cot, bg, acc, mixed, aog, bacc, bsum, upf, downf, lr, bn, grow,
-    gates, gf, g_send, g_got, g_sum, z_send, z_got, y_send, y_got, half, half_got, whole,
+    partial, gates, gf, g_send, g_got, g_sum, z_send, z_got, y_send, y_got, half, half_got, whole,
     send_sems, recv_sems, local_sems,
 ):
     place = Place()
@@ -276,12 +276,15 @@
     big = Gather("w", post, place, w_piece)
     small = Gather("p", post, place, pre_piece)
     own = pl.ds(pl.multiple_of(place.f * rows, rows), rows)
-    factor = amax[...].astype(jnp.float32)
+    per = gate.shape[0]
+    factor = feat[0:1, per : per + 1]
 
     pre[place.f, :rank, :] = up[...]
     for j in range(3):
         pre[place.f, rank:, j * 128 : (j + 1) * 128] = down[j * part : (j + 1) * part, :]
-    gates[0] = dot(feat[...], gate[...])[0:1]
+    partial[...] = dot(feat[:, :per].astype(jnp.bfloat16), gate[...])
+    sample = lax.div(place.dp * samples[0], samples[1])
+    gates[0] = partial[pl.ds(sample, 1), :]
 
     def scale(q):
         columns = pl.ds(pl.multiple_of(q * quarter, 128), quarter)
@@ -484,37 +487,66 @@
         store.wait()
 
 
+def hand_over(mixed, aog, dn, up, mixed_out, aog_out, dn_out, up_out, mixed_v, aog_v, dn_v, up_v, sems):
+    steps = []
+    for source, held, target, parts in (
+        (mixed, mixed_v, mixed_out, 4),
+        (aog, aog_v, aog_out, 2),
+        (dn, dn_v, dn_out, 1),
+        (up, up_v, up_out, 1),
+    ):
+        size = source.shape[0] // parts
+        for i in range(parts):
+            at, n = pl.ds(i * size, size), 2 * len(steps)
+            steps.append(
+                (
+                    pltpu.make_async_copy(source.at[at], held.at[at], sems.at[n]),
+                    pltpu.make_async_copy(held.at[at], target.at[at], sems.at[n + 1]),
+                )
+            )
+    for fetch, _ in steps:
+        fetch.start()
+    for fetch, store in steps:
+        fetch.wait()
+        store.start()
+    for _, store in steps:
+        store.wait()
+
+
 def fused(x, cot, codes, amax, down, up, gate, timesteps):
     tokens, inner = x.shape
     width, rank = cot.shape[1], up.shape[0]
     rows = codes.shape[0]
     dp_count, fsdp_count = lax.axis_size("dp"), lax.axis_size("fsdp")
     per = gate.shape[0]
-    sample = (lax.axis_index("dp") * fsdp_count) * tokens // PATCHES
-    chosen = jnp.arange(timesteps.shape[0], dtype=jnp.int32) == sample
-    step = jnp.sum(jnp.where(chosen, timesteps, 0)).astype(jnp.float32)
-    number = lax.axis_index("fsdp") * per + jnp.arange(per, dtype=jnp.int32)
+    shape = (timesteps.shape[0], 2 * per)
+    column = lax.broadcasted_iota(jnp.int32, shape, 1)
+    number = lax.axis_index("fsdp") * per + column
     half_freq = FREQ // 2
     frequency = jnp.exp(
         -math.log(10000.0) * (number % half_freq).astype(jnp.float32) / half_freq
     )
-    angle = step * frequency
-    feat = jnp.where(number < half_freq, jnp.cos(angle), jnp.sin(angle)).astype(jnp.bfloat16)
-    feat = jnp.broadcast_to(feat[None, :], (16, per))
+    angle = timesteps.astype(jnp.float32)[:, None] * frequency
+    feat = jnp.where(number < half_freq, jnp.cos(angle), jnp.sin(angle))
+    feat = jnp.where(column < per, feat, amax.astype(jnp.float32)[:, None])
     gradient_scale = (tokens * dp_count * fsdp_count) ** (-0.5)
     bf, f32 = jnp.bfloat16, jnp.float32
     quarter, hrows = width // 4, rows // 2
     vmem = pl.BlockSpec(memory_space=pltpu.VMEM)
     hbm = pl.BlockSpec(memory_space=pl.ANY)
-    return pl.pallas_call(
-        functools.partial(kernel, (gradient_scale, adapter_scale_factor * gradient_scale)),
+    results = pl.pallas_call(
+        functools.partial(
+            kernel,
+            (gradient_scale, adapter_scale_factor * gradient_scale),
+            (fsdp_count * tokens, PATCHES),
+        ),
         out_shape=(
             jax.ShapeDtypeStruct((tokens, width), bf),
             jax.ShapeDtypeStruct((tokens, inner), bf),
             jax.ShapeDtypeStruct((rows, rank), f32),
             jax.ShapeDtypeStruct((rank, up.shape[1]), f32),
         ),
-        in_specs=[hbm, hbm] + [vmem] * 6,
+        in_specs=[hbm, hbm] + [vmem] * 5,
         out_specs=(hbm, hbm, vmem, vmem),
         scratch_shapes=[
             pltpu.VMEM((4, inner, quarter), bf),
@@ -532,6 +564,7 @@
             pltpu.VMEM((tokens, rank), bf),
             pltpu.VMEM((tokens, rank), bf),
             pltpu.VMEM((1, width), f32),
+            pltpu.VMEM((timesteps.shape[0], width), f32),
             pltpu.VMEM((6, 1, width), f32),
             pltpu.VMEM((8, rows, up.shape[1]), f32),
             pltpu.VMEM((8, hrows, up.shape[1]), bf),
@@ -551,7 +584,16 @@
         compiler_params=pltpu.CompilerParams(
             collective_id=0, has_side_effects=True, vmem_limit_bytes=56 * 1024 * 1024
         ),
-    )(x, cot, codes, amax[None, :], down, up, gate, feat)
+    )(x, cot, codes, down, up, gate, feat)
+    return pl.pallas_call(
+        hand_over,
+        out_shape=tuple(jax.ShapeDtypeStruct(r.shape, r.dtype) for r in results),
+        in_specs=[hbm] * 4,
+        out_specs=(hbm,) * 4,
+        scratch_shapes=[pltpu.VMEM(r.shape, r.dtype) for r in results]
+        + [pltpu.SemaphoreType.DMA((16,))],
+        compiler_params=pltpu.CompilerParams(vmem_limit_bytes=60 * 1024 * 1024),
+    )(*results)
 
 
 def fits(mesh):

time: 75.8 us -> 72.2 us (0.953)
  local copies, waits for them, and re-layouts: 5.54 us -> 0 us
  Pallas kernels: 66.7 us -> 69.3 us
    unnamed x10 -> x0, local copies, waits for them, and re-layouts: 4.94 us -> none
    pallas_call x0 -> x1, Pallas kernels: none -> 2.62 us  [fused(): pl.pallas_call(hand_over, out_shape=tuple((jax.ShapeDtypeStruct(r.shape,...]
    reduce_sum x1 -> x0, other arithmetic: 1.29 us -> none  [fused(): step = jnp.sum(jnp.where(chosen, timesteps, 0)).astype(jnp.float32)]
where the time goes in v6:
time: 72.2 us; the launch traced here: 71.9 us
  Pallas kernels  69.3 us (96%)
  other arithmetic  1.37 us (2%)
  between operations  1.31 us (2%)
    pallas_call x1, Pallas kernels, fused(): pl.pallas_call(functools.partial(kernel, (gradient_scale, adapter_scale_f...  66.6 us
    pallas_call x1, Pallas kernels, fused(): pl.pallas_call(hand_over, out_shape=tuple((jax.ShapeDtypeStruct(r.shape,...  2.62 us

profile of v6, /device:TPU:0, one launch (start us, length us, event | category | flops | bytes accessed | tf_op | source)
XLA Modules:
  0.0 71.9 jit_solution(1209296080596112047)
XLA Ops:
  1.3 0.7 convert_element_type.7
  2.0 0.7 select_select_fusion.feat
  2.7 66.6 %shard_map.111 = (bf16[256,3072]{1,0:T(8,128)(2,1)}, bf16[256,1536]{1,0:T(8,128)(2,1)}, f32[192,128]{1,0:T(8,128)}, f32[128,384]{1,0:T(8,128)}) custom-call(bf16[256,1536]{1,0:T(8,128)(2,1)} %x_hbm.1, bf16[256,3072]{1,0:T(8,128)(2,1)} %cot_hbm.1, bf16[192,3072]{1,0:T(8,128)(2,1)} %codes.1, bf16[192,128]{1,0:T(8,128)(2,1)} %down.1, bf16[128,384]{1,0:T(8,128)(2,1)} %up.1, ...), custom_call_target="tpu_custom_call" | custom-call | tf_op jit(solution)/shard_map/pallas_call | solution.py:537
  69.3 2.6 %shard_map.112 = (bf16[256,3072]{1,0:T(8,128)(2,1)}, bf16[256,1536]{1,0:T(8,128)(2,1)}, f32[192,128]{1,0:T(8,128)}, f32[128,384]{1,0:T(8,128)}) custom-call(bf16[256,3072]{1,0:T(8,128)(2,1)} %get-tuple-element.8.mixed, bf16[256,1536]{1,0:T(8,128)(2,1)} %get-tuple-element.9.aog, f32[192,128]{1,0:T(8,128)} %get-tuple-element.10.dn, ...), custom_call_target="tpu_custom_call" | custom-call | tf_op jit(solution)/shard_map/pallas_call | solution.py:588
  (3 shorter events, 0.0 us)
